TPU v7x, 32 devices: a whole 2x2x4 slice. The times are simulated.
32 devices in a mesh: space: 4 (over x, core), snap: 8 (over z, y).
Axes of the slice: x: 2, y: 2, z: 4, core: 2. Of those that a mesh axis runs over, the one named last changes fastest.
Arguments:
- velocity: bfloat16 [64, 3, 8, 32, 128], P('snap', None, 'space'), may hold values from -40 to 40
- block_id: int32 [8, 32, 128], P('space'), may hold values from 0 to 7
- metric: float32 [8, 3], replicated, may hold values from 0.5 to 2
- leaf_rot: float32 [8, 8, 16], P('snap'), may hold values from -2 to 2
- merge_rot: float32 [7, 32, 16], replicated, may hold values from -1 to 1
- merge_order: int32 [7], replicated, may hold values from 0 to 1
- ref_cell: int32 [16], replicated, may hold values from 0 to 98303
Outputs:
- modes: float32 [16, 3, 8, 4096], P(None, None, 'space', 'snap')
All inputs are finite; a program needn't handle non-finite values.
Results may differ from a plain program's by a relative error of at most 0.0003.
Values may be sent and summed in bfloat16 or wider, within the bound.
A program may use at most 64 MiB of HBM per device.

v0:
```python
import jax
import jax.numpy as jnp
from jax import lax
from jax.sharding import PartitionSpec as P

HIGHEST = lax.Precision.HIGHEST


def padded(cells, sides, width):
    for axis, dim in sides:
        count = lax.axis_size(axis)
        ends = count - 1
        head = lax.slice_in_dim(cells, 0, width, axis=dim)
        tail = lax.slice_in_dim(cells, cells.shape[dim] - width, cells.shape[dim], axis=dim)
        cells = jnp.concatenate(
            [
                lax.ppermute(tail, axis, [(i, (i + 1) % count) for i in range(ends)]),
                cells,
                lax.ppermute(head, axis, [((i + 1) % count, i) for i in range(ends)]),
            ],
            axis=dim,
        )
    return cells


def from_partner(value, axis, apart):
    mask = 2**apart
    pairs = [(source, source ^ mask) for source in range(lax.axis_size(axis))]
    return lax.ppermute(value, axis, pairs)


def matmul(left, right):
    return jnp.dot(left, right, precision=HIGHEST, preferred_element_type=jnp.float32)


def along_x(field, spacing):
    return spacing[0] * (jnp.roll(field, -1, axis=2) - jnp.roll(field, 1, axis=2)) * 0.5


def along_z(field, spacing):
    return spacing[2] * (jnp.roll(field, -1, axis=3) - jnp.roll(field, 1, axis=3)) * 0.5


def ortho_factor(gram_total, rank):
    scale = (jnp.trace(gram_total) + 1e-06) / rank
    return 1.5 * jnp.eye(rank, dtype=jnp.float32) - 0.5 * gram_total / scale


def local(velocity, block_id, metric, leaf_rot, merge_rot, merge_order, ref_cell):
    snaps_here, _, rows_y, cells_x, cells_z = velocity.shape
    rank = leaf_rot.shape[2]
    blocks_count = metric.shape[0]
    onehot = (
        block_id[None] == jnp.arange(blocks_count, dtype=jnp.int32)[:, None, None, None]
    ).astype(jnp.float32)
    spacing = jnp.einsum("bxyz,bk->kxyz", onehot, metric, precision=HIGHEST)
    vel_uw = velocity[:, 0::2]
    extended = padded(vel_uw, (("space", 2),), 1).astype(jnp.float32)
    wall_diff = spacing[1] * (extended[:, :, 2:] - extended[:, :, :-2]) * 0.5
    vel_full = velocity.astype(jnp.float32)
    vel_u = vel_full[:, 0]
    vel_v = vel_full[:, 1]
    vel_w = vel_full[:, 2]
    omega_x = wall_diff[:, 1] - along_z(vel_v, spacing)
    omega_y = along_z(vel_u, spacing) - along_x(vel_w, spacing)
    omega_z = along_x(vel_v, spacing) - wall_diff[:, 0]
    omega = jnp.stack([omega_x, omega_y, omega_z], axis=1).reshape(snaps_here, -1)
    own_block = matmul(leaf_rot[0].T, omega)
    snap_count = lax.axis_size("snap")
    depth = snap_count.bit_length() - 1
    snap_index = lax.axis_index("snap")
    space_index = lax.axis_index("space")
    plane = cells_x * cells_z
    rows_total = rows_y * lax.axis_size("space")
    cells_all = 3 * rows_total * plane
    comp_of = ref_cell // (rows_total * plane)
    rest = ref_cell % (rows_total * plane)
    row_of = rest // plane - space_index * rows_y
    width = plane // snap_count
    inside = ((row_of >= 0) & (row_of < rows_y)).astype(jnp.float32)
    local_ref = jnp.clip(
        comp_of * rows_y * plane + row_of * plane + rest % plane, 0, 3 * rows_y * plane - 1
    )
    sign_value = None
    norm_sq = None
    for tree_level in range(depth):
        final_level = tree_level == depth - 1
        node_id = snap_count - (snap_count >> tree_level) + (snap_index >> tree_level + 1)
        rotation = lax.dynamic_index_in_dim(merge_rot, node_id, 0, keepdims=False)
        order_bit = lax.dynamic_index_in_dim(merge_order, node_id, 0, keepdims=False)
        position = snap_index >> tree_level & 1
        own_first = position == order_bit
        rot_top = rotation[:rank]
        rot_bottom = rotation[rank:]
        rot_own = jnp.where(own_first, rot_top, rot_bottom)
        rot_partner = jnp.where(own_first, rot_bottom, rot_top)
        partner = from_partner(own_block, "snap", tree_level)
        merged = matmul(rot_own.T, own_block) + matmul(rot_partner.T, partner)
        gram_total = lax.psum(matmul(merged, merged.T), "space")
        factor = ortho_factor(gram_total, rank)
        own_block = matmul(factor.T, merged)
        if final_level:
            picked = jnp.take_along_axis(own_block, local_ref[:, None], axis=1)[:, 0] * inside
            sign_value = lax.psum(picked, "space")
            norm_sq = jnp.sum(factor * matmul(gram_total, factor), axis=0)
    floor_value = 0.5 * jnp.sqrt(norm_sq / cells_all + 1e-06)
    sign = sign_value / jnp.maximum(jnp.abs(sign_value), floor_value)
    modes_full = (own_block * sign[:, None]).reshape(rank, 3, rows_y, plane)
    return lax.dynamic_slice_in_dim(modes_full, snap_index * width, width, 3)


def solution(mesh):
    placed = (
        P("snap", None, "space", None, None),
        P("space", None, None),
        P(),
        P("snap", None, None),
        P(),
        P(),
        P(),
    )
    return jax.shard_map(
        local, mesh=mesh, in_specs=placed, out_specs=P(None, None, "space", "snap"), check_vma=False
    )
```

profile of v0, /device:TPU:0, one launch (start us, length us, event | category | flops | bytes accessed | tf_op | source)
XLA Modules:
  0.0 239.6 jit_solution(6601143907909217434)
XLA Ops:
  1.7 3.0 %collective-permute-start = (bf16[8,2,1,32,128]{4,3,2,1,0:T(8,128)(2,1)}, bf16[8,2,1,32,128]{4,3,2,1,0:T(8,128)(2,1)}, u32[]{:S(2)}, u32[]{:S(2)}) collective-permute-start(bf16[8,2,1,32,128]{4,3,2,1,0:T(8,128)(2,1)} %get-tuple-element.28), channel_id=1, source_target_pairs={{0,8},{8,16},{16,24},{1,9},{9,17},{17,25},{2,10},{10,18},{18,26},{... | collective-permute-start | bytes 393224 | tf_op jit(solution)/shard_map/ppermute | solution.py:17
  6.0 1.8 copy.43
  8.3 2.1 slice_bitcast_fusion.7
  10.3 2.6 %fusion.95 = (f32[8,2,1,128]{2,0,3,1:T(8,128)}, f32[8,2,1,128]{2,0,3,1:T(8,128)}, f32[8,2,1,128]{2,0,3,1:T(8,128)}, f32[8,2,1,128]{2,0,3,1:T(8,128)}) fusion(f32[8,2,32,128]{2,0,3,1:T(8,128)S(1)} %get-tuple-element.7, f32[8,2,32,128]{2,0,3,1:T(8,128)S(1)} %get-tuple-element.9), kind=kLoop, calls=%fused_computation.150 | loop fusion | bytes 65536 | tf_op jit(solution)/shard_map/jit(_roll_static)/slice | solution.py:37
  12.9 1.6 slice_bitcast_fusion
  18.4 2.2 copy.51
  20.6 2.3 copy.48
  22.9 2.3 copy.44
  25.2 2.2 copy.47
  27.4 1.6 copy.55
  29.0 1.6 copy.52
  30.6 1.6 copy.58
  32.1 1.6 copy.61
  33.7 2.3 copy.63
  41.3 1.7 fusion.1
  43.0 2.4 %collective-permute-start.2 = (f32[16,24576]{1,0:T(8,128)S(1)}, f32[16,24576]{1,0:T(8,128)}, u32[]{:S(2)}, u32[]{:S(2)}) collective-permute-start(f32[16,24576]{1,0:T(8,128)S(1)} %bitcast.95), channel_id=1, source_target_pairs={{0,1},{1,0},{2,3},{3,2},{4,5},{5,4},{6,7},{7,6},{8,9},{9,8},{10,11... | collective-permute-start | bytes 4718600 | tf_op jit(solution)/shard_map/ppermute | solution.py:29
  48.2 31.2 %collective-permute-done.2 = f32[16,24576]{1,0:T(8,128)} collective-permute-done((f32[16,24576]{1,0:T(8,128)S(1)}, f32[16,24576]{1,0:T(8,128)}, u32[]{:S(2)}, u32[]{:S(2)}) %collective-permute-start.2) | collective-permute-done | bytes 1572896 | tf_op jit(solution)/shard_map/ppermute | solution.py:29
  79.4 2.9 %convolution_add_fusion.2 = f32[16,24576]{1,0:T(8,128)S(1)} fusion(f32[16,24576]{1,0:T(8,128)S(1)} %fusion.21, f32[16,24576]{1,0:T(8,128)} %collective-permute-done.2, f32[7,32,16]{1,2,0:T(8,128)S(1)} %copy-done.9, s32[]{:T(128)S(6)} %select_n.117, s32[]{:T(128)S(6)} %add.90, pred[]{:T(512)S(6)} %eq.47), kind=kOutput, calls=%fused_computation.3 | convolution fusion | flops 75890944 | bytes 4734985 | tf_op jit(solution)/shard_map/dot_general | solution.py:33
  82.3 2.4 %fusion.100 = f32[16,16]{1,0:T(8,128)S(1)} fusion(f32[16,24576]{1,0:T(8,128)S(1)} %convolution_add_fusion.2), kind=kOutput, calls=%fused_computation.155 | convolution fusion | flops 75497472 | bytes 1573888 | tf_op jit(solution)/shard_map/dot_general | solution.py:33
  84.8 7.5 %psum.28 = f32[16,16]{1,0:T(8,128)S(1)} all-reduce(f32[16,16]{1,0:T(8,128)S(1)} %fusion.100), channel_id=1, replica_groups=mesh['space'=4,'snap'=8] {'space'}, use_global_device_ids=true, to_apply=%region_0.1 | all-reduce | flops 256 | bytes 2048 | tf_op jit(solution)/shard_map/psum | solution.py:99
  93.4 1.5 fusion.16
  94.9 1.6 collective-permute-start.3
  98.6 32.9 %collective-permute-done.3 = f32[16,24576]{1,0:T(8,128)} collective-permute-done((f32[16,24576]{1,0:T(8,128)S(1)}, f32[16,24576]{1,0:T(8,128)}, u32[]{:S(2)}, u32[]{:S(2)}) %collective-permute-start.3) | collective-permute-done | bytes 1572896 | tf_op jit(solution)/shard_map/ppermute | solution.py:29
  131.5 2.9 %convolution_add_fusion.1 = f32[16,24576]{1,0:T(8,128)S(1)} fusion(f32[16,24576]{1,0:T(8,128)S(1)} %fusion.23, f32[16,24576]{1,0:T(8,128)} %collective-permute-done.3, f32[7,32,16]{1,2,0:T(8,128)S(1)} %copy-done.9, s32[]{:T(128)S(6)} %select_n.113, s32[]{:T(128)S(6)} %add.90, pred[]{:T(512)S(6)} %eq.46), kind=kOutput, calls=%fused_computation.2 | convolution fusion | flops 75890944 | bytes 4734985 | tf_op jit(solution)/shard_map/dot_general | solution.py:33
  134.4 2.2 fusion.101
  136.7 6.0 %psum.29 = f32[16,16]{1,0:T(8,128)S(1)} all-reduce(f32[16,16]{1,0:T(8,128)S(1)} %fusion.101), channel_id=1, replica_groups=mesh['space'=4,'snap'=8] {'space'}, use_global_device_ids=true, to_apply=%region_2.3 | all-reduce | flops 256 | bytes 2048 | tf_op jit(solution)/shard_map/psum | solution.py:99
  145.4 2.6 %collective-permute-start.4 = (f32[16,24576]{1,0:T(8,128)S(1)}, f32[16,24576]{1,0:T(8,128)}, u32[]{:S(2)}, u32[]{:S(2)}) collective-permute-start(f32[16,24576]{1,0:T(8,128)S(1)} %fusion.17), channel_id=1, source_target_pairs={{0,4},{1,5},{2,6},{3,7},{4,0},{5,1},{6,2},{7,3},{8,12},{9,13},{10,... | collective-permute-start | bytes 4718600 | tf_op jit(solution)/shard_map/ppermute | solution.py:29
  150.2 66.0 %collective-permute-done.4 = f32[16,24576]{1,0:T(8,128)} collective-permute-done((f32[16,24576]{1,0:T(8,128)S(1)}, f32[16,24576]{1,0:T(8,128)}, u32[]{:S(2)}, u32[]{:S(2)}) %collective-permute-start.4) | collective-permute-done | bytes 1572896 | tf_op jit(solution)/shard_map/ppermute | solution.py:29
  216.3 2.9 %convolution_add_fusion = f32[16,24576]{1,0:T(8,128)S(1)} fusion(f32[16,24576]{1,0:T(8,128)S(1)} %fusion.25, f32[16,24576]{1,0:T(8,128)} %collective-permute-done.4, f32[7,32,16]{1,2,0:T(8,128)S(1)} %copy-done.9, s32[]{:T(128)S(6)} %select_n.109, s32[]{:T(128)S(6)} %add.90, pred[]{:T(512)S(6)} %eq.45), kind=kOutput, calls=%fused_computation.1 | convolution fusion | flops 75890944 | bytes 4734985 | tf_op jit(solution)/shard_map/dot_general | solution.py:33
  219.2 2.1 fusion.102
  221.3 6.2 %psum.30 = f32[16,16]{1,0:T(8,128)S(1)} all-reduce(f32[16,16]{1,0:T(8,128)S(1)} %fusion.102), channel_id=1, replica_groups=mesh['space'=4,'snap'=8] {'space'}, use_global_device_ids=true, to_apply=%region_4.5 | all-reduce | flops 256 | bytes 2048 | tf_op jit(solution)/shard_map/psum | solution.py:99
  231.1 6.3 %psum.31 = f32[16]{0:T(128)S(1)} all-reduce(f32[16]{0:T(128)S(1)} %and_select_fusion.3), channel_id=1, replica_groups=mesh['space'=4,'snap'=8] {'space'}, use_global_device_ids=true, to_apply=%region_6.7 | all-reduce | flops 16 | bytes 128 | tf_op jit(solution)/shard_map/psum | solution.py:104
  (74 shorter events, 25.5 us)
Async XLA Ops:
  0.0 41.3 %copy-start = (f32[1,8,16]{2,1,0:T(8,128)S(1)}, f32[1,8,16]{2,1,0:T(8,128)}, u32[]{:S(2)}) copy-start(f32[1,8,16]{2,1,0:T(8,128)} %param.10) | copy-start | bytes 1540
  1.7 37.8 %collective-permute-start = (bf16[8,2,1,32,128]{4,3,2,1,0:T(8,128)(2,1)}, bf16[8,2,1,32,128]{4,3,2,1,0:T(8,128)(2,1)}, u32[]{:S(2)}, u32[]{:S(2)}) collective-permute-start(bf16[8,2,1,32,128]{4,3,2,1,0:T(8,128)(2,1)} %get-tuple-element.28), channel_id=1, source_target_pairs={{0,8},{8,16},{16,24},{1,9},{9,17},{17,25},{2,10},{10,18},{18,26},{... | collective-permute-start | bytes 393224 | tf_op jit(solution)/shard_map/ppermute | solution.py:17
  4.7 34.8 %collective-permute-start.1 = (bf16[8,2,1,32,128]{4,3,2,1,0:T(8,128)(2,1)}, bf16[8,2,1,32,128]{4,3,2,1,0:T(8,128)(2,1)}, u32[]{:S(2)}, u32[]{:S(2)}) collective-permute-start(bf16[8,2,1,32,128]{4,3,2,1,0:T(8,128)(2,1)} %get-tuple-element.29), channel_id=1, source_target_pairs={{8,0},{16,8},{24,16},{9,1},{17,9},{25,17},{10,2},{18,10},{26,18},{... | collective-permute-start | bytes 393224 | tf_op jit(solution)/shard_map/ppermute | solution.py:19
  12.9 1.7 copy-start.10
  12.9 1.7 copy-start.12
  37.1 0.9 copy-start.5
  37.1 1.0 copy-start.6
  39.4 1.4 copy-start.1
  39.4 1.4 copy-start.2
  39.4 1.4 copy-start.3
  39.5 1.4 copy-start.4
  39.5 1.4 copy-start.7
  39.5 1.4 copy-start.8
  41.2 4.2 %copy-start.11 = (s32[7]{0:T(128)S(1)}, s32[7]{0:T(128)}, u32[]{:S(2)}) copy-start(s32[7]{0:T(128)} %param.12) | copy-start | bytes 88
  41.2 5.5 %copy-start.9 = (f32[7,32,16]{1,2,0:T(8,128)S(1)}, f32[7,32,16]{1,2,0:T(8,128)}, u32[]{:S(2)}) copy-start(f32[7,32,16]{1,2,0:T(8,128)} %param.11) | copy-start | bytes 43012
  43.0 36.4 %collective-permute-start.2 = (f32[16,24576]{1,0:T(8,128)S(1)}, f32[16,24576]{1,0:T(8,128)}, u32[]{:S(2)}, u32[]{:S(2)}) collective-permute-start(f32[16,24576]{1,0:T(8,128)S(1)} %bitcast.95), channel_id=1, source_target_pairs={{0,1},{1,0},{2,3},{3,2},{4,5},{5,4},{6,7},{7,6},{8,9},{9,8},{10,11... | collective-permute-start | bytes 4718600 | tf_op jit(solution)/shard_map/ppermute | solution.py:29
  94.9 36.6 %collective-permute-start.3 = (f32[16,24576]{1,0:T(8,128)S(1)}, f32[16,24576]{1,0:T(8,128)}, u32[]{:S(2)}, u32[]{:S(2)}) collective-permute-start(f32[16,24576]{1,0:T(8,128)S(1)} %fusion.16), channel_id=1, source_target_pairs={{0,2},{1,3},{2,0},{3,1},{4,6},{5,7},{6,4},{7,5},{8,10},{9,11},{10,... | collective-permute-start | bytes 4718600 | tf_op jit(solution)/shard_map/ppermute | solution.py:29
  143.9 4.8 %copy-start.13 = (s32[16]{0:T(128)S(1)}, s32[16]{0:T(128)}, u32[]{:S(2)}) copy-start(s32[16]{0:T(128)} %param.13) | copy-start | bytes 196
  145.4 70.8 %collective-permute-start.4 = (f32[16,24576]{1,0:T(8,128)S(1)}, f32[16,24576]{1,0:T(8,128)}, u32[]{:S(2)}, u32[]{:S(2)}) collective-permute-start(f32[16,24576]{1,0:T(8,128)S(1)} %fusion.17), channel_id=1, source_target_pairs={{0,4},{1,5},{2,6},{3,7},{4,0},{5,1},{6,2},{7,3},{8,12},{9,13},{10,... | collective-permute-start | bytes 4718600 | tf_op jit(solution)/shard_map/ppermute | solution.py:29
where the time goes:
time: 240 us
  waiting for transfers between devices  130 us (54%)
  local copies, waits for them, and re-layouts  36.8 us (15%)
  matrix products  26.6 us (11%)
  blocking collectives  26 us (11%)
  starting transfers between devices  10.8 us (4%)
  other arithmetic  5.12 us (2%)
  between operations  4.15 us (2%)
    ppermute x3, waiting for transfers between devices, from_partner(): return lax.ppermute(value, axis, pairs)  130 us
    dot_general x14, matrix products, matmul(): jnp.dot(left, right, precision=HIGHEST, preferred_element_type=jnp.float32)  26.3 us
    psum x3, blocking collectives, local(): gram_total = lax.psum(matmul(merged, merged.T), 'space')  19.8 us
    concatenate x6, local copies, waits for them, and re-layouts, along_z(): jnp.roll(field, 1, axis=3)  8.3 us
    ppermute x3, starting transfers between devices, from_partner(): return lax.ppermute(value, axis, pairs)  6.55 us
    psum x1, blocking collectives, local(): sign_value = lax.psum(picked, 'space')  6.26 us
    concatenate x4, local copies, waits for them, and re-layouts, along_z(): jnp.roll(field, -1, axis=3) - jnp.roll(field, 1, axis=3)  6.26 us
    slice x3, local copies, waits for them, and re-layouts, along_x(): jnp.roll(field, 1, axis=2)  5.7 us
  transfers between devices with their start and end apart: 5, of which 3 were waited for; matrix products, arithmetic and copies ran while one was open for 16% of the time, Pallas kernels for 0%

commit v1 on v0

v1 whole, which is shorter than its diff:
```python
import functools

import jax
import jax.numpy as jnp
from jax import lax
from jax.experimental import pallas as pl
from jax.experimental.pallas import tpu as pltpu
from jax.sharding import PartitionSpec as P

HIGHEST = lax.Precision.HIGHEST
MESH = pl.DeviceIdType.MESH
F32 = jnp.float32
BF16 = jnp.bfloat16


def exact(left, right, dims=((1,), (0,))):
    return lax.dot_general(left, right, (dims, ((), ())), precision=HIGHEST, preferred_element_type=F32)


def product(left, right, dims=((1,), (0,))):
    return lax.dot_general(left, right, (dims, ((), ())), preferred_element_type=F32)


def iota(shape, dim):
    return lax.broadcasted_iota(jnp.int32, shape, dim)


def ortho_factor(gram, rank):
    size = gram.shape[0]
    eye = iota(gram.shape, 0) == iota(gram.shape, 1)
    same = iota(gram.shape, 0) // rank == iota(gram.shape, 1) // rank
    diagonal = jnp.sum(jnp.where(eye, gram, 0.0), axis=0, keepdims=True)
    if size > rank:
        spread = jnp.broadcast_to(diagonal, (8, size))
        trace = exact(spread, same.astype(F32))[:1]
    else:
        trace = jnp.sum(diagonal, axis=1, keepdims=True)
    scale = (trace + 1e-06) / rank
    return 1.5 * eye.astype(F32) - jnp.where(same, 0.5 * gram / scale, 0.0)


def kernel(
    dims,
    vel_ref, block_ref, metric_ref, leaf_ref, rot_ref, order_ref, cell_ref, out_ref,
    velf, send_u, send_vw, recv_u, recv_vw, stage, halo, lead, spacing, parts_hi, parts_lo,
    gram_own, gram_space, gram_snap, gram_all,
    sem_u_s, sem_u_r, sem_vw_s, sem_vw_r, sem_lead_s, sem_lead_r, sem_halo_s, sem_halo_r,
    sem_a_s, sem_a_r, sem_b_s, sem_b_r, sem_c_s, sem_c_r,
):
    groups, spaces = dims
    here, _, rows_y, cells_x, cells_z = vel_ref.shape
    rank = leaf_ref.shape[2]
    blocks = metric_ref.shape[0]
    total = groups * here
    width_x = cells_x // groups
    me = lax.axis_index("snap")
    sp = lax.axis_index("space")
    first_x = me * width_x

    def peer(step):
        return lax.rem(me + step, groups)

    def mate(step):
        return lax.rem(sp + step, spaces)

    barrier = pltpu.get_barrier_semaphore()
    for step in range(1, spaces):
        pl.semaphore_signal(barrier, inc=1, device_id={"space": mate(step)}, device_id_type=MESH)

    def greet(step, carry):
        pl.semaphore_signal(barrier, inc=1, device_id={"snap": peer(step)}, device_id_type=MESH)
        return carry

    lax.fori_loop(1, groups, greet, 0)

    stretch = 3 * rows_y * cells_x

    def widen(snap, carry):
        start = pl.multiple_of(snap * stretch, stretch)
        velf[pl.ds(start, stretch), :] = vel_ref[snap].reshape(stretch, cells_z).astype(F32)
        return carry

    lax.fori_loop(0, here, widen, 0)

    def tile(comp, x):
        pieces = [
            velf[pl.ds((comp * rows_y + y) * cells_x + x, here, stride=stretch), :]
            for y in range(rows_y)
        ]
        return jnp.concatenate(pieces, axis=0).astype(BF16)

    def regroup(x, carry):
        send_u[x] = tile(0, x)
        send_vw[0, x + 1] = tile(1, x)
        send_vw[1, x + 1] = tile(2, x)
        return carry

    lax.fori_loop(0, cells_x, regroup, 0, unroll=4)
    for comp in range(2):
        send_vw[comp, 0] = send_vw[comp, cells_x]
        send_vw[comp, cells_x + 1] = send_vw[comp, 1]

    lead_width = lead.shape[2]
    turn = rot_ref[me // 2]
    pick = (order_ref[me // 2] - me % 2).astype(F32)
    pick = pick * pick
    turn_own = turn[:rank] * (1.0 - pick) + turn[rank:] * pick
    lead_own = exact(leaf_ref[0], turn_own)
    repeat = (iota((rank, lead_width), 1) % rank == iota((rank, lead_width), 0)).astype(F32)
    lead_wide = exact(lead_own, repeat)
    lead[me] = jnp.where(iota(lead_wide.shape, 1) // rank == me // 2, lead_wide, 0.0)

    pl.semaphore_wait(barrier, groups + spaces - 2)

    def copies(step):
        to = peer(step)
        start = to * width_x
        return (
            pltpu.make_async_remote_copy(
                send_vw.at[:, pl.ds(start, width_x + 2)], recv_vw.at[me],
                sem_vw_s.at[step], sem_vw_r.at[me], device_id={"snap": to}, device_id_type=MESH,
            ),
            pltpu.make_async_remote_copy(
                send_u.at[pl.ds(start, width_x)], recv_u.at[me],
                sem_u_s.at[step], sem_u_r.at[me], device_id={"snap": to}, device_id_type=MESH,
            ),
            pltpu.make_async_remote_copy(
                lead.at[me], lead.at[me],
                sem_lead_s.at[step], sem_lead_r.at[me], device_id={"snap": to}, device_id_type=MESH,
            ),
        )

    def arrivals(source):
        return (
            pltpu.make_async_remote_copy(
                recv_vw.at[source], recv_vw.at[source],
                sem_vw_s.at[0], sem_vw_r.at[source], device_id={"snap": source}, device_id_type=MESH,
            ),
            pltpu.make_async_remote_copy(
                recv_u.at[source], recv_u.at[source],
                sem_u_s.at[0], sem_u_r.at[source], device_id={"snap": source}, device_id_type=MESH,
            ),
            pltpu.make_async_remote_copy(
                lead.at[source], lead.at[source],
                sem_lead_s.at[0], sem_lead_r.at[source], device_id={"snap": source}, device_id_type=MESH,
            ),
        )

    def launch(step, carry):
        for copy in copies(step):
            copy.start()
        return carry

    lax.fori_loop(1, groups, launch, 0)

    def halo_copy(side, group):
        to = sp + 1 if side == 0 else sp - 1
        return pltpu.make_async_remote_copy(
            stage.at[side, group], halo.at[side, group],
            sem_halo_s.at[side, group], sem_halo_r.at[side, group],
            device_id={"space": to}, device_id_type=MESH,
        )

    def forward(group):
        for x in range(width_x):
            u_here = recv_u[group, x].astype(F32)
            w_here = recv_vw[group, 1, x + 1].astype(F32)
            stage[1, group, x] = jnp.concatenate([u_here[:here], w_here[:here]], axis=0).astype(BF16)
            stage[0, group, x] = jnp.concatenate([u_here[-here:], w_here[-here:]], axis=0).astype(BF16)

        @pl.when(sp < spaces - 1)
        def _():
            halo_copy(0, group).start()

        @pl.when(sp > 0)
        def _():
            halo_copy(1, group).start()

    recv_u[me] = send_u[pl.ds(first_x, width_x)]
    recv_vw[me] = send_vw[:, pl.ds(first_x, width_x + 2)]
    forward(me)

    @pl.when(sp == 0)
    def _():
        halo[0] = jnp.zeros(halo.shape[1:], BF16)

    @pl.when(sp == spaces - 1)
    def _():
        halo[1] = jnp.zeros(halo.shape[1:], BF16)

    for y in range(rows_y):
        for x in range(width_x):
            ids = block_ref[y, pl.ds(first_x + x, 1), :]
            for axis in range(3):
                value = jnp.zeros((1, cells_z), F32)
                for block in range(blocks):
                    value = jnp.where(ids == block, metric_ref[block, axis], value)
                spacing[axis, y, pl.ds(x, 1), :] = 0.5 * value

    plane = cells_x * cells_z
    parts_hi[pl.ds(total, parts_hi.shape[0] - total), :] = jnp.zeros(
        (parts_hi.shape[0] - total, parts_hi.shape[1]), BF16
    )
    parts_lo[pl.ds(total, parts_lo.shape[0] - total), :] = jnp.zeros(
        (parts_lo.shape[0] - total, parts_lo.shape[1]), BF16
    )
    row = iota((rank, cells_z), 0)
    wanted = jnp.zeros((rank, cells_z), jnp.int32)
    for mode in range(rank):
        wanted = jnp.where(row == mode, cell_ref[mode], wanted)
    for comp in range(3):
        for y in range(rows_y):
            for x in range(width_x):
                base = ((comp * rows_y * spaces + sp * rows_y + y) * cells_x + first_x + x) * cells_z
                hit = jnp.where(wanted == base + iota((rank, cells_z), 1), 1.0, 0.0)
                column = ((comp * rows_y + y) * width_x + x) * cells_z
                parts_hi[pl.ds(total, rank), pl.ds(column, cells_z)] = hit.astype(BF16)

    depth = groups.bit_length() - 1
    turns = []
    for level in range(1, depth):
        nodes = groups >> level + 1
        stacked = []
        for k in range(nodes):
            node = groups - (groups >> level) + k
            plain = rot_ref[node]
            swapped = jnp.concatenate([plain[rank:], plain[:rank]], axis=0)
            flag = order_ref[node].astype(F32)
            stacked.append(plain * (1.0 - flag) + swapped * flag)
        stacked = stacked[0] if nodes == 1 else jnp.concatenate(stacked, axis=0)
        if nodes > 1:
            shape = (rank, rank * nodes)
            copy_out = (iota(shape, 1) % rank == iota(shape, 0)).astype(F32)
            stacked = exact(stacked, copy_out)
            stacked = jnp.where(
                iota(stacked.shape, 0) // (2 * rank) == iota(stacked.shape, 1) // rank, stacked, 0.0
            )
        turns.append(stacked)

    def receive(step, carry):
        source = lax.rem(me - step + groups, groups)
        for copy in arrivals(source):
            copy.wait_recv()
        forward(source)
        return carry

    lax.fori_loop(1, groups, receive, 0)

    def split_store(start, column, value):
        high = value.astype(BF16)
        low = (value - high.astype(F32)).astype(BF16)
        parts_hi[pl.ds(start, 2 * here), pl.ds(column, cells_z)] = high
        parts_lo[pl.ds(start, 2 * here), pl.ds(column, cells_z)] = low

    def wait_halo(group):
        @pl.when(sp > 0)
        def _():
            halo_copy(0, group).wait_recv()

        @pl.when(sp < spaces - 1)
        def _():
            halo_copy(1, group).wait_recv()

    def curl(pair, carry):
        pair_groups = (2 * pair, 2 * pair + 1)
        start = pl.multiple_of(pair * 2 * here, 2 * here)
        for group in pair_groups:
            wait_halo(group)

        def load(ref, *index):
            both = [ref[(group, *index)].astype(F32) for group in pair_groups]
            return [
                jnp.concatenate([item[y * here:(y + 1) * here] for item in both], axis=0)
                for y in range(rows_y)
            ]

        def load_halo(side, x):
            both = [halo[side, group, x].astype(F32) for group in pair_groups]
            return [jnp.concatenate([item[c * here:(c + 1) * here] for item in both], axis=0) for c in range(2)]

        def along_z(field):
            return pltpu.roll(field, cells_z - 1, 1) - pltpu.roll(field, 1, 1)

        for x in range(width_x):
            u_at = load(recv_u, x)
            v_at = load(recv_vw, 0, x + 1)
            w_at = load(recv_vw, 1, x + 1)
            v_ends = load(recv_vw, 0, x), load(recv_vw, 0, x + 2)
            w_ends = load(recv_vw, 1, x), load(recv_vw, 1, x + 2)
            below = load_halo(0, x)
            above = load_halo(1, x)
            for y in range(rows_y):
                hx, hy, hz = (spacing[axis, y, pl.ds(x, 1), :] for axis in range(3))
                u_down = u_at[y - 1] if y > 0 else below[0]
                w_down = w_at[y - 1] if y > 0 else below[1]
                u_up = u_at[y + 1] if y < rows_y - 1 else above[0]
                w_up = w_at[y + 1] if y < rows_y - 1 else above[1]
                omega = (
                    hy * (w_up - w_down) - hz * along_z(v_at[y]),
                    hz * along_z(u_at[y]) - hx * (w_ends[1][y] - w_ends[0][y]),
                    hx * (v_ends[1][y] - v_ends[0][y]) - hy * (u_up - u_down),
                )
                for comp in range(3):
                    split_store(start, ((comp * rows_y + y) * width_x + x) * cells_z, omega[comp])
        return carry

    lax.fori_loop(0, groups // 2, curl, 0)

    high = parts_hi[:total]
    low = parts_lo[:total]
    last = ((1,), (1,))
    gram_own[...] = (
        product(high, parts_hi[...], last) + product(low, parts_hi[...], last) + product(high, parts_lo[...], last)
    ).reshape(gram_own.shape)

    def copy_a(step):
        to = mate(step)
        return pltpu.make_async_remote_copy(
            gram_own.at[to], gram_space.at[step], sem_a_s.at[step], sem_a_r.at[step],
            device_id={"space": to}, device_id_type=MESH,
        )

    for step in range(1, spaces):
        copy_a(step).start()
    lead_all = lead[...].reshape(total, lead_width)[:, :rank * groups // 2]
    part = gram_own[sp]
    for step in range(1, spaces):
        copy_a(step).wait_recv()
        part = part + gram_space[step]
    gram_snap[0] = part

    def copy_b(step):
        return pltpu.make_async_remote_copy(
            gram_snap.at[0], gram_snap.at[step], sem_b_s.at[step], sem_b_r.at[step],
            device_id={"snap": peer(step)}, device_id_type=MESH,
        )

    def start_b(step, carry):
        copy_b(step).start()
        return carry

    def finish_b(step, carry):
        copy_b(step).wait_recv()
        return carry + gram_snap[step]

    lax.fori_loop(1, groups, start_b, 0)
    gram_all[sp] = lax.fori_loop(1, groups, finish_b, part)

    def copy_c(step, owner):
        return pltpu.make_async_remote_copy(
            gram_all.at[owner], gram_all.at[owner], sem_c_s.at[step], sem_c_r.at[step],
            device_id={"space": mate(step)}, device_id_type=MESH,
        )

    for step in range(1, spaces):
        copy_c(step, sp).start()
    for step in range(1, spaces):
        copy_c(step, lax.rem(sp - step + spaces, spaces)).wait_recv()
    summed = gram_all[...].reshape(total, gram_all.shape[2])

    first = ((0,), (0,))
    entries = summed[:, total:total + rank]
    maps = lead_all
    gram = exact(maps, exact(summed[:, :total], maps), first)
    for turn in turns:
        step_map = exact(ortho_factor(gram, rank), turn)
        gram = exact(step_map, exact(gram, step_map), first)
        maps = exact(maps, step_map)
    factor = ortho_factor(gram, rank)
    value = jnp.sum(factor * exact(maps, entries, first), axis=0, keepdims=True)
    norm_sq = jnp.sum(factor * exact(gram, factor), axis=0, keepdims=True)
    cells_all = 3 * rows_y * spaces * plane
    floor = 0.5 * jnp.sqrt(norm_sq / cells_all + 1e-06)
    sign = value / jnp.maximum(jnp.abs(value), floor)
    mix = exact(factor * sign, maps, ((0,), (1,)))
    mix_high = mix.astype(BF16)
    mix_low = (mix - mix_high.astype(F32)).astype(BF16)
    both = product(jnp.concatenate([mix_high, mix_low], axis=0), high)
    out_ref[...] = both[:rank] + both[rank:] + product(mix_high, low)

    def finish(step, carry):
        for copy in copies(step):
            copy.wait_send()
        copy_b(step).wait_send()
        return carry

    lax.fori_loop(1, groups, finish, 0)
    for step in range(1, spaces):
        copy_a(step).wait_send()
        copy_c(step, sp).wait_send()

    def finish_halo(group, carry):
        @pl.when(sp < spaces - 1)
        def _():
            halo_copy(0, group).wait_send()

        @pl.when(sp > 0)
        def _():
            halo_copy(1, group).wait_send()

        return carry

    lax.fori_loop(0, groups, finish_halo, 0)


def padded(size, unit):
    return -(-size // unit) * unit


def local(velocity, block_id, metric, leaf_rot, merge_rot, merge_order, ref_cell):
    here, _, rows_y, cells_x, cells_z = velocity.shape
    rank = leaf_rot.shape[2]
    groups = lax.axis_size("snap")
    spaces = lax.axis_size("space")
    total = groups * here
    width_x = cells_x // groups
    tile_rows = rows_y * here
    cells = 3 * rows_y * width_x * cells_z
    gram_width = padded(total + rank, 128)
    share = total // spaces
    lead_width = padded(rank * groups // 2, 128)
    vmem = pl.BlockSpec(memory_space=pltpu.VMEM)
    smem = pl.BlockSpec(memory_space=pltpu.SMEM)
    dma = pltpu.SemaphoreType.DMA
    modes = pl.pallas_call(
        functools.partial(kernel, (groups, spaces)),
        out_shape=jax.ShapeDtypeStruct((rank, cells), F32),
        in_specs=[vmem, vmem, smem, vmem, vmem, smem, smem],
        out_specs=vmem,
        scratch_shapes=[
            pltpu.VMEM((here * 3 * rows_y * cells_x, cells_z), F32),
            pltpu.VMEM((cells_x, tile_rows, cells_z), BF16),
            pltpu.VMEM((2, cells_x + 2, tile_rows, cells_z), BF16),
            pltpu.VMEM((groups, width_x, tile_rows, cells_z), BF16),
            pltpu.VMEM((groups, 2, width_x + 2, tile_rows, cells_z), BF16),
            pltpu.VMEM((2, groups, width_x, 2 * here, cells_z), BF16),
            pltpu.VMEM((2, groups, width_x, 2 * here, cells_z), BF16),
            pltpu.VMEM((groups, here, lead_width), F32),
            pltpu.VMEM((3, rows_y, width_x, cells_z), F32),
            pltpu.VMEM((gram_width, cells), BF16),
            pltpu.VMEM((gram_width, cells), BF16),
            pltpu.VMEM((spaces, share, gram_width), F32),
            pltpu.VMEM((spaces, share, gram_width), F32),
            pltpu.VMEM((groups, share, gram_width), F32),
            pltpu.VMEM((spaces, share, gram_width), F32),
        ]
        + [dma((groups,))] * 6
        + [dma((2, groups))] * 2
        + [dma((spaces,))] * 2
        + [dma((groups,))] * 2
        + [dma((spaces,))] * 2,
        compiler_params=pltpu.CompilerParams(
            collective_id=0, has_side_effects=True, vmem_limit_bytes=32 * 1024 * 1024
        ),
    )(velocity, block_id, metric, leaf_rot, merge_rot, merge_order, ref_cell)
    return modes.reshape(rank, 3, rows_y, width_x * cells_z)


def solution(mesh):
    placed = (
        P("snap", None, "space", None, None),
        P("space", None, None),
        P(),
        P("snap", None, None),
        P(),
        P(),
        P(),
    )
    return jax.shard_map(
        local, mesh=mesh, in_specs=placed, out_specs=P(None, None, "space", "snap"), check_vma=False
    )
```

time: 240 us -> 41.9 us (0.17)
  waiting for transfers between devices: 130 us -> 0 us
  Pallas kernels: 0 us -> 38 us
  local copies, waits for them, and re-layouts: 36.8 us -> 3.56 us
  matrix products: 26.6 us -> 0 us
  blocking collectives: 26 us -> 0 us
  starting transfers between devices: 10.8 us -> 0 us
  other arithmetic: 5.12 us -> 0 us
  between operations: 4.15 us -> 0.06 us
    ppermute x5 -> x0, waiting for transfers between devices: 130 us -> none  [the longest x3 130 us: from_partner(): return lax.ppermute(value, axis, pairs)]
    pallas_call x0 -> x1, Pallas kernels: none -> 38 us  [local(): pl.pallas_call(functools.partial(kernel, (groups, spaces)), out_shape=jax...]
    dot_general x15 -> x0, matrix products: 26.6 us -> none  [the longest x14 26.3 us: matmul(): jnp.dot(left, right, precision=HIGHEST, preferred_element_type=jnp.float32)]
    psum x4 -> x0, blocking collectives: 26 us -> none  [the longest x3 19.8 us: local(): gram_total = lax.psum(matmul(merged, merged.T), 'space')]
    concatenate x19 -> x0, local copies, waits for them, and re-layouts: 20.5 us -> none  [the longest x6 8.3 us: along_z(): jnp.roll(field, 1, axis=3)]
    ppermute x5 -> x0, starting transfers between devices: 10.8 us -> none  [the longest x3 6.55 us: from_partner(): return lax.ppermute(value, axis, pairs)]
    slice x8 -> x0, local copies, waits for them, and re-layouts: 10.6 us -> none  [the longest x3 5.7 us: along_x(): jnp.roll(field, 1, axis=2)]
  transfers between devices with their start and end apart: 5 -> 0, of which waited for: 3 -> 0; matrix products, arithmetic and copies ran while one was open for 16% -> 0% of each run, Pallas kernels for 0% -> 0%
where the time goes in v1:
time: 41.9 us; the launch traced here: 41.6 us
  Pallas kernels  38 us (91%)
  local copies, waits for them, and re-layouts  3.56 us (8%)
    pallas_call x1, Pallas kernels, local(): pl.pallas_call(functools.partial(kernel, (groups, spaces)), out_shape=jax...  38 us
    unnamed x12, local copies, waits for them, and re-layouts  2.72 us
    reshape x1, local copies, waits for them, and re-layouts, local(): return modes.reshape(rank, 3, rows_y, width_x * cells_z)  0.84 us

profile of v1, /device:TPU:0, one launch (start us, length us, event | category | flops | bytes accessed | tf_op | source)
XLA Modules:
  0.0 41.6 jit_solution(5610479804060451659)
XLA Ops:
  0.0 0.8 %copy.8.metric_ref = f32[8,3]{1,0:T(8,128)S(1)} copy(f32[8,3]{0,1:T(4,128)} %param.9) | data formatting | bytes 192 | tf_op args[2]
  0.8 0.0 copy-start.1
  0.8 0.0 copy-start.2
  0.8 0.0 copy-start.3
  0.8 0.0 copy-start.4
  0.8 1.0 %copy.9.rot_ref = f32[7,32,16]{2,1,0:T(8,128)S(1)} copy(f32[7,32,16]{1,2,0:T(8,128)} %param.11) | data formatting | bytes 28672 | tf_op args[4]
  1.7 0.0 copy-done.1
  1.7 0.0 copy-done.2
  1.8 0.0 copy-done.3
  1.8 0.0 copy-done.4
  1.8 0.0 copy-start
  1.8 1.0 %copy-done = bf16[8,3,2,32,128]{4,3,2,1,0:T(8,128)(2,1)S(1)} copy-done((bf16[8,3,2,32,128]{4,3,2,1,0:T(8,128)(2,1)S(1)}, bf16[8,3,2,32,128]{4,3,2,1,0:T(8,128)(2,1)}, u32[]{:S(2)}) %copy-start) | copy-done | bytes 393240
  2.8 38.0 %shard_map.73 = f32[16,3072]{1,0:T(8,128)S(1)} custom-call(bf16[8,3,2,32,128]{4,3,2,1,0:T(8,128)(2,1)S(1)} %copy-done, s32[2,32,128]{2,1,0:T(8,128)S(1)} %copy-done.1, f32[8,3]{1,0:T(8,128)S(1)} %copy.8.metric_ref, f32[1,8,16]{2,1,0:T(8,128)S(1)} %copy-done.2, f32[7,32,16]{2,1,0:T(8,128)S(1)} %copy.9.rot_ref, s32[7]{0:T(128)S(1)} %copy-done.3, s32[16]{0:T(128)S(1)} %copy-done.4), custom_call_target="tpu_custom_call" | custom-call | tf_op jit(solution)/shard_map/pallas_call | solution.py:425
  40.8 0.8 %reshape.3 = f32[16,3,2,512]{3,2,1,0:T(2,128)} reshape(f32[16,3072]{1,0:T(8,128)S(1)} %shard_map.73) | data formatting | bytes 393216 | tf_op jit(solution)/shard_map/reshape | solution.py:456
Async XLA Ops:
  0.8 1.0 %copy-start.1 = (s32[2,32,128]{2,1,0:T(8,128)S(1)}, s32[2,32,128]{2,1,0:T(8,128)}, u32[]{:S(2)}) copy-start(s32[2,32,128]{2,1,0:T(8,128)} %block_ref.1) | copy-start | bytes 98308
  0.8 1.0 %copy-start.2 = (f32[1,8,16]{2,1,0:T(8,128)S(1)}, f32[1,8,16]{2,1,0:T(8,128)}, u32[]{:S(2)}) copy-start(f32[1,8,16]{2,1,0:T(8,128)} %leaf_ref.1) | copy-start | bytes 1540
  0.8 1.0 %copy-start.3 = (s32[7]{0:T(128)S(1)}, s32[7]{0:T(128)}, u32[]{:S(2)}) copy-start(s32[7]{0:T(128)} %order_ref.1) | copy-start | bytes 88
  0.8 1.0 %copy-start.4 = (s32[16]{0:T(128)S(1)}, s32[16]{0:T(128)}, u32[]{:S(2)}) copy-start(s32[16]{0:T(128)} %cell_ref.1) | copy-start | bytes 196
  1.8 1.0 %copy-start = (bf16[8,3,2,32,128]{4,3,2,1,0:T(8,128)(2,1)S(1)}, bf16[8,3,2,32,128]{4,3,2,1,0:T(8,128)(2,1)}, u32[]{:S(2)}) copy-start(bf16[8,3,2,32,128]{4,3,2,1,0:T(8,128)(2,1)} %vel_ref.1) | copy-start | bytes 1179652

commit v2 on v1

--- a/solution.py
+++ b/solution.py
@@ -21,6 +21,21 @@
     return lax.dot_general(left, right, (dims, ((), ())), preferred_element_type=F32)
 
 
+def split(value):
+    high = value.astype(BF16)
+    return high, (value - high.astype(F32)).astype(BF16)
+
+
+def close(left, right, dims=((1,), (0,))):
+    left_high, left_low = split(left)
+    right_high, right_low = split(right)
+    return (
+        product(left_high, right_high, dims)
+        + product(left_high, right_low, dims)
+        + product(left_low, right_high, dims)
+    )
+
+
 def iota(shape, dim):
     return lax.broadcasted_iota(jnp.int32, shape, dim)
 
@@ -30,33 +45,37 @@
     eye = iota(gram.shape, 0) == iota(gram.shape, 1)
     same = iota(gram.shape, 0) // rank == iota(gram.shape, 1) // rank
     diagonal = jnp.sum(jnp.where(eye, gram, 0.0), axis=0, keepdims=True)
-    if size > rank:
-        spread = jnp.broadcast_to(diagonal, (8, size))
-        trace = exact(spread, same.astype(F32))[:1]
-    else:
-        trace = jnp.sum(diagonal, axis=1, keepdims=True)
+    node_of = iota((1, size), 1) // rank
+    trace = jnp.zeros((1, size), F32)
+    for node in range(size // rank):
+        own = jnp.where(node_of == node, diagonal, 0.0)
+        trace = jnp.where(node_of == node, jnp.sum(own, axis=1, keepdims=True), trace)
     scale = (trace + 1e-06) / rank
     return 1.5 * eye.astype(F32) - jnp.where(same, 0.5 * gram / scale, 0.0)
 
 
 def kernel(
     dims,
-    vel_ref, block_ref, metric_ref, leaf_ref, rot_ref, order_ref, cell_ref, out_ref,
-    velf, send_u, send_vw, recv_u, recv_vw, stage, halo, lead, spacing, parts_hi, parts_lo,
+    vel_hbm, block_ref, metric_ref, leaf_ref, rot_ref, order_ref, cell_ref, out_ref,
+    vel_ref, velf, send_u, send_vw, recv_u, recv_vw, stage, halo, lead, spacing, parts,
     gram_own, gram_space, gram_snap, gram_all,
-    sem_u_s, sem_u_r, sem_vw_s, sem_vw_r, sem_lead_s, sem_lead_r, sem_halo_s, sem_halo_r,
+    sem_vel, sem_u_s, sem_u_r, sem_vw_s, sem_vw_r, sem_lead_s, sem_lead_r, sem_halo_s, sem_halo_r,
     sem_a_s, sem_a_r, sem_b_s, sem_b_r, sem_c_s, sem_c_r,
 ):
     groups, spaces = dims
     here, _, rows_y, cells_x, cells_z = vel_ref.shape
     rank = leaf_ref.shape[2]
-    blocks = metric_ref.shape[0]
+    blocks = metric_ref.shape[1]
     total = groups * here
     width_x = cells_x // groups
     me = lax.axis_index("snap")
     sp = lax.axis_index("space")
     first_x = me * width_x
 
+    half = groups // 2
+    load_velocity = pltpu.make_async_copy(vel_hbm, vel_ref, sem_vel)
+    load_velocity.start()
+
     def peer(step):
         return lax.rem(me + step, groups)
 
@@ -80,6 +99,7 @@
         velf[pl.ds(start, stretch), :] = vel_ref[snap].reshape(stretch, cells_z).astype(F32)
         return carry
 
+    load_velocity.wait()
     lax.fori_loop(0, here, widen, 0)
 
     def tile(comp, x):
@@ -89,44 +109,38 @@
         ]
         return jnp.concatenate(pieces, axis=0).astype(BF16)
 
-    def regroup(x, carry):
-        send_u[x] = tile(0, x)
-        send_vw[0, x + 1] = tile(1, x)
-        send_vw[1, x + 1] = tile(2, x)
-        return carry
-
-    lax.fori_loop(0, cells_x, regroup, 0, unroll=4)
-    for comp in range(2):
-        send_vw[comp, 0] = send_vw[comp, cells_x]
-        send_vw[comp, cells_x + 1] = send_vw[comp, 1]
-
-    lead_width = lead.shape[2]
-    turn = rot_ref[me // 2]
-    pick = (order_ref[me // 2] - me % 2).astype(F32)
-    pick = pick * pick
-    turn_own = turn[:rank] * (1.0 - pick) + turn[rank:] * pick
-    lead_own = exact(leaf_ref[0], turn_own)
-    repeat = (iota((rank, lead_width), 1) % rank == iota((rank, lead_width), 0)).astype(F32)
-    lead_wide = exact(lead_own, repeat)
-    lead[me] = jnp.where(iota(lead_wide.shape, 1) // rank == me // 2, lead_wide, 0.0)
+    def target(step):
+        mine = me // half
+        far = (1 - mine) * half + lax.rem(me + step, half)
+        near = mine * half + lax.rem(me + step, half)
+        return jnp.where(step < half, far, near)
+
+    def regroup(to, u_to, vw_to):
+        start = to * width_x
+        for x in range(width_x):
+            u_to[x] = tile(0, start + x)
+        for comp in range(2):
+            for x in range(width_x + 2):
+                vw_to[comp, x] = tile(comp + 1, lax.rem(start + x + cells_x - 1, cells_x))
 
     pl.semaphore_wait(barrier, groups + spaces - 2)
 
+    def lead_copy(step):
+        return pltpu.make_async_remote_copy(
+            lead.at[me], lead.at[me],
+            sem_lead_s.at[step], sem_lead_r.at[me], device_id={"snap": peer(step)}, device_id_type=MESH,
+        )
+
     def copies(step):
-        to = peer(step)
-        start = to * width_x
+        to = target(step)
         return (
             pltpu.make_async_remote_copy(
-                send_vw.at[:, pl.ds(start, width_x + 2)], recv_vw.at[me],
+                send_vw.at[step], recv_vw.at[me],
                 sem_vw_s.at[step], sem_vw_r.at[me], device_id={"snap": to}, device_id_type=MESH,
             ),
             pltpu.make_async_remote_copy(
-                send_u.at[pl.ds(start, width_x)], recv_u.at[me],
+                send_u.at[step], recv_u.at[me],
                 sem_u_s.at[step], sem_u_r.at[me], device_id={"snap": to}, device_id_type=MESH,
-            ),
-            pltpu.make_async_remote_copy(
-                lead.at[me], lead.at[me],
-                sem_lead_s.at[step], sem_lead_r.at[me], device_id={"snap": to}, device_id_type=MESH,
             ),
         )
 
@@ -147,11 +161,30 @@
         )
 
     def launch(step, carry):
+        regroup(target(step), send_u.at[step], send_vw.at[step])
         for copy in copies(step):
             copy.start()
         return carry
 
-    lax.fori_loop(1, groups, launch, 0)
+    lax.fori_loop(0, half, launch, 0)
+    lax.fori_loop(half + 1, groups, launch, 0)
+    regroup(me, recv_u.at[me], recv_vw.at[me])
+
+    lead_width = lead.shape[2]
+    turn = rot_ref[me // 2].T
+    pick = (order_ref[me // 2] - me % 2).astype(F32)
+    pick = pick * pick
+    turn_own = turn[:rank] * (1.0 - pick) + turn[rank:] * pick
+    lead_own = exact(leaf_ref[0], turn_own)
+    repeat = (iota((rank, lead_width), 1) % rank == iota((rank, lead_width), 0)).astype(F32)
+    lead_wide = exact(lead_own, repeat)
+    lead[me] = jnp.where(iota(lead_wide.shape, 1) // rank == me // 2, lead_wide, 0.0)
+
+    def launch_lead(step, carry):
+        lead_copy(step).start()
+        return carry
+
+    lax.fori_loop(1, groups, launch_lead, 0)
 
     def halo_copy(side, group):
         to = sp + 1 if side == 0 else sp - 1
@@ -176,10 +209,6 @@
         def _():
             halo_copy(1, group).start()
 
-    recv_u[me] = send_u[pl.ds(first_x, width_x)]
-    recv_vw[me] = send_vw[:, pl.ds(first_x, width_x + 2)]
-    forward(me)
-
     @pl.when(sp == 0)
     def _():
         halo[0] = jnp.zeros(halo.shape[1:], BF16)
@@ -194,16 +223,12 @@
             for axis in range(3):
                 value = jnp.zeros((1, cells_z), F32)
                 for block in range(blocks):
-                    value = jnp.where(ids == block, metric_ref[block, axis], value)
+                    value = jnp.where(ids == block, metric_ref[axis, block], value)
                 spacing[axis, y, pl.ds(x, 1), :] = 0.5 * value
 
     plane = cells_x * cells_z
-    parts_hi[pl.ds(total, parts_hi.shape[0] - total), :] = jnp.zeros(
-        (parts_hi.shape[0] - total, parts_hi.shape[1]), BF16
-    )
-    parts_lo[pl.ds(total, parts_lo.shape[0] - total), :] = jnp.zeros(
-        (parts_lo.shape[0] - total, parts_lo.shape[1]), BF16
-    )
+    rest = parts.shape[0] - 2 * total
+    parts[pl.ds(2 * total, rest), :] = jnp.zeros((rest, parts.shape[1]), BF16)
     row = iota((rank, cells_z), 0)
     wanted = jnp.zeros((rank, cells_z), jnp.int32)
     for mode in range(rank):
@@ -214,7 +239,7 @@
                 base = ((comp * rows_y * spaces + sp * rows_y + y) * cells_x + first_x + x) * cells_z
                 hit = jnp.where(wanted == base + iota((rank, cells_z), 1), 1.0, 0.0)
                 column = ((comp * rows_y + y) * width_x + x) * cells_z
-                parts_hi[pl.ds(total, rank), pl.ds(column, cells_z)] = hit.astype(BF16)
+                parts[pl.ds(2 * total, rank), pl.ds(column, cells_z)] = hit.astype(BF16)
 
     depth = groups.bit_length() - 1
     turns = []
@@ -223,7 +248,7 @@
         stacked = []
         for k in range(nodes):
             node = groups - (groups >> level) + k
-            plain = rot_ref[node]
+            plain = rot_ref[node].T
             swapped = jnp.concatenate([plain[rank:], plain[:rank]], axis=0)
             flag = order_ref[node].astype(F32)
             stacked.append(plain * (1.0 - flag) + swapped * flag)
@@ -237,20 +262,10 @@
             )
         turns.append(stacked)
 
-    def receive(step, carry):
-        source = lax.rem(me - step + groups, groups)
-        for copy in arrivals(source):
-            copy.wait_recv()
-        forward(source)
-        return carry
-
-    lax.fori_loop(1, groups, receive, 0)
-
     def split_store(start, column, value):
-        high = value.astype(BF16)
-        low = (value - high.astype(F32)).astype(BF16)
-        parts_hi[pl.ds(start, 2 * here), pl.ds(column, cells_z)] = high
-        parts_lo[pl.ds(start, 2 * here), pl.ds(column, cells_z)] = low
+        high, low = split(value)
+        parts[pl.ds(start, 2 * here), pl.ds(column, cells_z)] = low
+        parts[pl.ds(total + start, 2 * here), pl.ds(column, cells_z)] = high
 
     def wait_halo(group):
         @pl.when(sp > 0)
@@ -261,7 +276,7 @@
         def _():
             halo_copy(1, group).wait_recv()
 
-    def curl(pair, carry):
+    def curl(pair):
         pair_groups = (2 * pair, 2 * pair + 1)
         start = pl.multiple_of(pair * 2 * here, 2 * here)
         for group in pair_groups:
@@ -302,16 +317,40 @@
                 )
                 for comp in range(3):
                     split_store(start, ((comp * rows_y + y) * width_x + x) * cells_z, omega[comp])
-        return carry
-
-    lax.fori_loop(0, groups // 2, curl, 0)
-
-    high = parts_hi[:total]
-    low = parts_lo[:total]
-    last = ((1,), (1,))
-    gram_own[...] = (
-        product(high, parts_hi[...], last) + product(low, parts_hi[...], last) + product(high, parts_lo[...], last)
-    ).reshape(gram_own.shape)
+
+    def nth_pair(step):
+        quarter = max(half // 2, 1)
+        own = me // 2
+        side = own // quarter
+        near = side * quarter + lax.rem(own + step, quarter)
+        far = (1 - side) * quarter + lax.rem(own + step, quarter)
+        return jnp.where(step < quarter, near, far) if half > 1 else own
+
+    def pipeline(step, carry):
+        @pl.when(step < half)
+        def _():
+            for place in range(2):
+                source = 2 * nth_pair(step) + place
+
+                @pl.when(source != me)
+                def _():
+                    for copy in arrivals(source):
+                        copy.wait_recv()
+
+                forward(source)
+
+        @pl.when(step > 0)
+        def _():
+            curl(nth_pair(step - 1))
+
+        return carry
+
+    lax.fori_loop(0, half + 1, pipeline, 0)
+
+    both = product(parts[:2 * total], parts[total:], ((1,), (1,)))
+    crossed = both[:total, :total].T
+    gap = jnp.zeros((total, both.shape[1] - total), F32)
+    gram_own[...] = (both[:total] + both[total:] + jnp.concatenate([crossed, gap], axis=1)).reshape(gram_own.shape)
 
     def copy_a(step):
         to = mate(step)
@@ -358,33 +397,39 @@
         copy_c(step, lax.rem(sp - step + spaces, spaces)).wait_recv()
     summed = gram_all[...].reshape(total, gram_all.shape[2])
 
-    first = ((0,), (0,))
     entries = summed[:, total:total + rank]
     maps = lead_all
-    gram = exact(maps, exact(summed[:, :total], maps), first)
+    gram = close(maps.T, close(summed[:, :total], maps))
     for turn in turns:
-        step_map = exact(ortho_factor(gram, rank), turn)
-        gram = exact(step_map, exact(gram, step_map), first)
-        maps = exact(maps, step_map)
+        step_map = close(ortho_factor(gram, rank), turn)
+        gram = close(step_map.T, close(gram, step_map))
+        maps = close(maps, step_map)
     factor = ortho_factor(gram, rank)
-    value = jnp.sum(factor * exact(maps, entries, first), axis=0, keepdims=True)
-    norm_sq = jnp.sum(factor * exact(gram, factor), axis=0, keepdims=True)
+    value = jnp.sum(factor * close(maps.T, entries), axis=0, keepdims=True)
+    norm_sq = jnp.sum(factor * close(gram, factor), axis=0, keepdims=True)
     cells_all = 3 * rows_y * spaces * plane
     floor = 0.5 * jnp.sqrt(norm_sq / cells_all + 1e-06)
     sign = value / jnp.maximum(jnp.abs(value), floor)
-    mix = exact(factor * sign, maps, ((0,), (1,)))
-    mix_high = mix.astype(BF16)
-    mix_low = (mix - mix_high.astype(F32)).astype(BF16)
+    mix = close((factor * sign).T, maps, ((1,), (1,)))
+    mix_high, mix_low = split(mix)
+    high = parts[total:2 * total]
     both = product(jnp.concatenate([mix_high, mix_low], axis=0), high)
-    out_ref[...] = both[:rank] + both[rank:] + product(mix_high, low)
+    out_ref[...] = both[:rank] + both[rank:] + product(mix_high, parts[:total])
 
     def finish(step, carry):
         for copy in copies(step):
             copy.wait_send()
+        return carry
+
+    lax.fori_loop(0, half, finish, 0)
+    lax.fori_loop(half + 1, groups, finish, 0)
+
+    def finish_small(step, carry):
+        lead_copy(step).wait_send()
         copy_b(step).wait_send()
         return carry
 
-    lax.fori_loop(1, groups, finish, 0)
+    lax.fori_loop(1, groups, finish_small, 0)
     for step in range(1, spaces):
         copy_a(step).wait_send()
         copy_c(step, sp).wait_send()
@@ -425,25 +470,26 @@
     modes = pl.pallas_call(
         functools.partial(kernel, (groups, spaces)),
         out_shape=jax.ShapeDtypeStruct((rank, cells), F32),
-        in_specs=[vmem, vmem, smem, vmem, vmem, smem, smem],
+        in_specs=[pl.BlockSpec(memory_space=pltpu.HBM), vmem, smem, vmem, vmem, smem, smem],
         out_specs=vmem,
         scratch_shapes=[
+            pltpu.VMEM(velocity.shape, BF16),
             pltpu.VMEM((here * 3 * rows_y * cells_x, cells_z), F32),
-            pltpu.VMEM((cells_x, tile_rows, cells_z), BF16),
-            pltpu.VMEM((2, cells_x + 2, tile_rows, cells_z), BF16),
+            pltpu.VMEM((groups, width_x, tile_rows, cells_z), BF16),
+            pltpu.VMEM((groups, 2, width_x + 2, tile_rows, cells_z), BF16),
             pltpu.VMEM((groups, width_x, tile_rows, cells_z), BF16),
             pltpu.VMEM((groups, 2, width_x + 2, tile_rows, cells_z), BF16),
             pltpu.VMEM((2, groups, width_x, 2 * here, cells_z), BF16),
             pltpu.VMEM((2, groups, width_x, 2 * here, cells_z), BF16),
             pltpu.VMEM((groups, here, lead_width), F32),
             pltpu.VMEM((3, rows_y, width_x, cells_z), F32),
-            pltpu.VMEM((gram_width, cells), BF16),
-            pltpu.VMEM((gram_width, cells), BF16),
+            pltpu.VMEM((total + gram_width, cells), BF16),
             pltpu.VMEM((spaces, share, gram_width), F32),
             pltpu.VMEM((spaces, share, gram_width), F32),
             pltpu.VMEM((groups, share, gram_width), F32),
             pltpu.VMEM((spaces, share, gram_width), F32),
         ]
+        + [dma]
         + [dma((groups,))] * 6
         + [dma((2, groups))] * 2
         + [dma((spaces,))] * 2
@@ -452,7 +498,7 @@
         compiler_params=pltpu.CompilerParams(
             collective_id=0, has_side_effects=True, vmem_limit_bytes=32 * 1024 * 1024
         ),
-    )(velocity, block_id, metric, leaf_rot, merge_rot, merge_order, ref_cell)
+    )(velocity, block_id, metric.T, leaf_rot, jnp.swapaxes(merge_rot, 1, 2), merge_order, ref_cell)
     return modes.reshape(rank, 3, rows_y, width_x * cells_z)
 
 

time: 41.9 us -> 42.2 us (level)
  local copies, waits for them, and re-layouts: 3.56 us -> 4.79 us
  Pallas kernels: 38 us -> 37 us
    unnamed x12 -> x14, local copies, waits for them, and re-layouts: 2.72 us -> 3.94 us
    pallas_call x1, Pallas kernels: 38 us -> 37 us  [local(): pl.pallas_call(functools.partial(kernel, (groups, spaces)), out_shape=jax...]
where the time goes in v2:
time: 42.2 us; the launch traced here: 41.8 us
  Pallas kernels  37 us (88%)
  local copies, waits for them, and re-layouts  4.79 us (11%)
    pallas_call x1, Pallas kernels, local(): pl.pallas_call(functools.partial(kernel, (groups, spaces)), out_shape=jax...  37 us
    unnamed x14, local copies, waits for them, and re-layouts  3.94 us
    reshape x1, local copies, waits for them, and re-layouts, local(): return modes.reshape(rank, 3, rows_y, width_x * cells_z)  0.84 us

profile of v2, /device:TPU:0, one launch (start us, length us, event | category | flops | bytes accessed | tf_op | source)
XLA Modules:
  0.0 41.8 jit_solution(11935787001070770326)
XLA Ops:
  0.0 0.0 copy-start.4
  0.0 0.0 copy-start.5
  0.0 0.0 copy-start.6
  0.0 0.7 %copy-done.4 = f32[8,3]{0,1:T(4,128)S(1)} copy-done((f32[8,3]{0,1:T(4,128)S(1)}, f32[8,3]{0,1:T(4,128)}, u32[]{:S(2)}) %copy-start.4) | copy-done | bytes 120
  0.7 0.0 copy-done.5
  0.7 0.0 copy-done.6
  0.7 0.0 copy-start
  0.7 1.0 %copy-done = bf16[8,3,2,32,128]{4,3,2,1,0:T(8,128)(2,1)S(1)} copy-done((bf16[8,3,2,32,128]{4,3,2,1,0:T(8,128)(2,1)S(1)}, bf16[8,3,2,32,128]{4,3,2,1,0:T(8,128)(2,1)}, u32[]{:S(2)}) %copy-start) | copy-done | bytes 393240
  1.7 0.0 copy-start.1
  1.7 0.8 %copy-done.1 = f32[7,32,16]{1,2,0:T(8,128)S(1)} copy-done((f32[7,32,16]{1,2,0:T(8,128)S(1)}, f32[7,32,16]{1,2,0:T(8,128)}, u32[]{:S(2)}) %copy-start.1) | copy-done | bytes 14360
  2.5 0.0 copy-start.2
  2.5 0.8 %copy-done.2 = s32[2,32,128]{2,1,0:T(8,128)S(1)} copy-done((s32[2,32,128]{2,1,0:T(8,128)S(1)}, s32[2,32,128]{2,1,0:T(8,128)}, u32[]{:S(2)}) %copy-start.2) | copy-done | bytes 32792
  3.3 0.0 copy-start.3
  3.3 0.7 %copy-done.3 = f32[1,8,16]{2,1,0:T(8,128)S(1)} copy-done((f32[1,8,16]{2,1,0:T(8,128)S(1)}, f32[1,8,16]{2,1,0:T(8,128)}, u32[]{:S(2)}) %copy-start.3) | copy-done | bytes 536
  4.0 37.0 %shard_map.73 = f32[16,3072]{1,0:T(8,128)S(1)} custom-call(bf16[8,3,2,32,128]{4,3,2,1,0:T(8,128)(2,1)S(1)} %copy-done, s32[2,32,128]{2,1,0:T(8,128)S(1)} %copy-done.2, f32[3,8]{1,0:T(4,128)S(1)} %bitcast.3, f32[1,8,16]{2,1,0:T(8,128)S(1)} %copy-done.3, f32[7,16,32]{2,1,0:T(8,128)S(1)} %bitcast.2, s32[7]{0:T(128)S(1)} %copy-done.5, s32[16]{0:T(128)S(1)} %copy-done.6), custom_call_target="tpu_custom_call" | custom-call | tf_op jit(solution)/shard_map/pallas_call | solution.py:470
  41.0 0.8 %reshape.3 = f32[16,3,2,512]{3,2,1,0:T(2,128)} reshape(f32[16,3072]{1,0:T(8,128)S(1)} %shard_map.73) | data formatting | bytes 393216 | tf_op jit(solution)/shard_map/reshape | solution.py:502
Async XLA Ops:
  0.0 0.7 %copy-start.4 = (f32[8,3]{0,1:T(4,128)S(1)}, f32[8,3]{0,1:T(4,128)}, u32[]{:S(2)}) copy-start(f32[8,3]{0,1:T(4,128)} %param.9) | copy-start | bytes 292
  0.0 0.7 %copy-start.5 = (s32[7]{0:T(128)S(1)}, s32[7]{0:T(128)}, u32[]{:S(2)}) copy-start(s32[7]{0:T(128)} %order_ref.1) | copy-start | bytes 88
  0.0 0.7 %copy-start.6 = (s32[16]{0:T(128)S(1)}, s32[16]{0:T(128)}, u32[]{:S(2)}) copy-start(s32[16]{0:T(128)} %cell_ref.1) | copy-start | bytes 196
  0.7 1.0 %copy-start = (bf16[8,3,2,32,128]{4,3,2,1,0:T(8,128)(2,1)S(1)}, bf16[8,3,2,32,128]{4,3,2,1,0:T(8,128)(2,1)}, u32[]{:S(2)}) copy-start(bf16[8,3,2,32,128]{4,3,2,1,0:T(8,128)(2,1)} %vel_hbm.1) | copy-start | bytes 1179652
  1.7 0.8 %copy-start.1 = (f32[7,32,16]{1,2,0:T(8,128)S(1)}, f32[7,32,16]{1,2,0:T(8,128)}, u32[]{:S(2)}) copy-start(f32[7,32,16]{1,2,0:T(8,128)} %param.11) | copy-start | bytes 43012
  2.5 0.8 %copy-start.2 = (s32[2,32,128]{2,1,0:T(8,128)S(1)}, s32[2,32,128]{2,1,0:T(8,128)}, u32[]{:S(2)}) copy-start(s32[2,32,128]{2,1,0:T(8,128)} %block_ref.1) | copy-start | bytes 98308
  3.3 0.7 %copy-start.3 = (f32[1,8,16]{2,1,0:T(8,128)S(1)}, f32[1,8,16]{2,1,0:T(8,128)}, u32[]{:S(2)}) copy-start(f32[1,8,16]{2,1,0:T(8,128)} %leaf_ref.1) | copy-start | bytes 1540

commit v3 on v2

--- a/solution.py
+++ b/solution.py
@@ -24,16 +24,6 @@
 def split(value):
     high = value.astype(BF16)
     return high, (value - high.astype(F32)).astype(BF16)
-
-
-def close(left, right, dims=((1,), (0,))):
-    left_high, left_low = split(left)
-    right_high, right_low = split(right)
-    return (
-        product(left_high, right_high, dims)
-        + product(left_high, right_low, dims)
-        + product(left_low, right_high, dims)
-    )
 
 
 def iota(shape, dim):
@@ -56,10 +46,11 @@
 
 def kernel(
     dims,
-    vel_hbm, block_ref, metric_ref, leaf_ref, rot_ref, order_ref, cell_ref, out_ref,
-    vel_ref, velf, send_u, send_vw, recv_u, recv_vw, stage, halo, lead, spacing, parts,
+    vel_hbm, block_hbm, metric_hbm, leaf_hbm, rot_hbm, order_hbm, cell_hbm, out_ref,
+    vel_ref, block_ref, metric_ref, leaf_ref, rot_ref, order_ref, cell_ref,
+    velf, send, recv, stage, halo, lead, spacing, parts,
     gram_own, gram_space, gram_snap, gram_all,
-    sem_vel, sem_u_s, sem_u_r, sem_vw_s, sem_vw_r, sem_lead_s, sem_lead_r, sem_halo_s, sem_halo_r,
+    sem_in, sem_main_s, sem_main_r, sem_x_s, sem_x_r, sem_lead_s, sem_lead_r, sem_halo_s, sem_halo_r,
     sem_a_s, sem_a_r, sem_b_s, sem_b_r, sem_c_s, sem_c_r,
 ):
     groups, spaces = dims
@@ -73,8 +64,15 @@
     first_x = me * width_x
 
     half = groups // 2
-    load_velocity = pltpu.make_async_copy(vel_hbm, vel_ref, sem_vel)
-    load_velocity.start()
+    loads = [
+        pltpu.make_async_copy(source, place, sem_in.at[index])
+        for index, (source, place) in enumerate((
+            (vel_hbm, vel_ref), (block_hbm, block_ref), (metric_hbm, metric_ref), (leaf_hbm, leaf_ref),
+            (rot_hbm, rot_ref), (order_hbm, order_ref), (cell_hbm, cell_ref),
+        ))
+    ]
+    for load in loads:
+        load.start()
 
     def peer(step):
         return lax.rem(me + step, groups)
@@ -99,7 +97,7 @@
         velf[pl.ds(start, stretch), :] = vel_ref[snap].reshape(stretch, cells_z).astype(F32)
         return carry
 
-    load_velocity.wait()
+    loads[0].wait()
     lax.fori_loop(0, here, widen, 0)
 
     def tile(comp, x):
@@ -115,13 +113,11 @@
         near = mine * half + lax.rem(me + step, half)
         return jnp.where(step < half, far, near)
 
-    def regroup(to, u_to, vw_to):
+    def regroup(to, place):
         start = to * width_x
-        for x in range(width_x):
-            u_to[x] = tile(0, start + x)
-        for comp in range(2):
-            for x in range(width_x + 2):
-                vw_to[comp, x] = tile(comp + 1, lax.rem(start + x + cells_x - 1, cells_x))
+        for comp in range(3):
+            for x in range(width_x):
+                place[comp, x] = tile(comp, start + x)
 
     pl.semaphore_wait(barrier, groups + spaces - 2)
 
@@ -131,28 +127,25 @@
             sem_lead_s.at[step], sem_lead_r.at[me], device_id={"snap": peer(step)}, device_id_type=MESH,
         )
 
-    def copies(step):
-        to = target(step)
-        return (
-            pltpu.make_async_remote_copy(
-                send_vw.at[step], recv_vw.at[me],
-                sem_vw_s.at[step], sem_vw_r.at[me], device_id={"snap": to}, device_id_type=MESH,
-            ),
-            pltpu.make_async_remote_copy(
-                send_u.at[step], recv_u.at[me],
-                sem_u_s.at[step], sem_u_r.at[me], device_id={"snap": to}, device_id_type=MESH,
-            ),
+    def main_copy(step):
+        return pltpu.make_async_remote_copy(
+            send.at[step], recv.at[me, :, pl.ds(1, width_x)],
+            sem_main_s.at[step], sem_main_r.at[me], device_id={"snap": target(step)}, device_id_type=MESH,
+        )
+
+    def x_copy(side, group):
+        from_row, to_row = (width_x, 0) if side == 0 else (1, width_x + 1)
+        to = peer(1) if side == 0 else peer(groups - 1)
+        return pltpu.make_async_remote_copy(
+            recv.at[group, pl.ds(1, 2), from_row], recv.at[group, pl.ds(1, 2), to_row],
+            sem_x_s.at[side, group], sem_x_r.at[side, group], device_id={"snap": to}, device_id_type=MESH,
         )
 
     def arrivals(source):
         return (
             pltpu.make_async_remote_copy(
-                recv_vw.at[source], recv_vw.at[source],
-                sem_vw_s.at[0], sem_vw_r.at[source], device_id={"snap": source}, device_id_type=MESH,
-            ),
-            pltpu.make_async_remote_copy(
-                recv_u.at[source], recv_u.at[source],
-                sem_u_s.at[0], sem_u_r.at[source], device_id={"snap": source}, device_id_type=MESH,
+                recv.at[source, :, pl.ds(1, width_x)], recv.at[source, :, pl.ds(1, width_x)],
+                sem_main_s.at[0], sem_main_r.at[source], device_id={"snap": source}, device_id_type=MESH,
             ),
             pltpu.make_async_remote_copy(
                 lead.at[source], lead.at[source],
@@ -161,14 +154,15 @@
         )
 
     def launch(step, carry):
-        regroup(target(step), send_u.at[step], send_vw.at[step])
-        for copy in copies(step):
-            copy.start()
+        regroup(target(step), send.at[step])
+        main_copy(step).start()
         return carry
 
     lax.fori_loop(0, half, launch, 0)
     lax.fori_loop(half + 1, groups, launch, 0)
-    regroup(me, recv_u.at[me], recv_vw.at[me])
+    regroup(me, recv.at[me, :, pl.ds(1, width_x)])
+    for load in loads[1:]:
+        load.wait()
 
     lead_width = lead.shape[2]
     turn = rot_ref[me // 2].T
@@ -195,9 +189,11 @@
         )
 
     def forward(group):
+        for side in range(2):
+            x_copy(side, group).start()
         for x in range(width_x):
-            u_here = recv_u[group, x].astype(F32)
-            w_here = recv_vw[group, 1, x + 1].astype(F32)
+            u_here = recv[group, 0, x + 1].astype(F32)
+            w_here = recv[group, 2, x + 1].astype(F32)
             stage[1, group, x] = jnp.concatenate([u_here[:here], w_here[:here]], axis=0).astype(BF16)
             stage[0, group, x] = jnp.concatenate([u_here[-here:], w_here[-here:]], axis=0).astype(BF16)
 
@@ -268,6 +264,9 @@
         parts[pl.ds(total + start, 2 * here), pl.ds(column, cells_z)] = high
 
     def wait_halo(group):
+        for side in range(2):
+            x_copy(side, group).wait_recv()
+
         @pl.when(sp > 0)
         def _():
             halo_copy(0, group).wait_recv()
@@ -297,11 +296,11 @@
             return pltpu.roll(field, cells_z - 1, 1) - pltpu.roll(field, 1, 1)
 
         for x in range(width_x):
-            u_at = load(recv_u, x)
-            v_at = load(recv_vw, 0, x + 1)
-            w_at = load(recv_vw, 1, x + 1)
-            v_ends = load(recv_vw, 0, x), load(recv_vw, 0, x + 2)
-            w_ends = load(recv_vw, 1, x), load(recv_vw, 1, x + 2)
+            u_at = load(recv, 0, x + 1)
+            v_at = load(recv, 1, x + 1)
+            w_at = load(recv, 2, x + 1)
+            v_ends = load(recv, 1, x), load(recv, 1, x + 2)
+            w_ends = load(recv, 2, x), load(recv, 2, x + 2)
             below = load_halo(0, x)
             above = load_halo(1, x)
             for y in range(rows_y):
@@ -318,34 +317,37 @@
                 for comp in range(3):
                     split_store(start, ((comp * rows_y + y) * width_x + x) * cells_z, omega[comp])
 
-    def nth_pair(step):
-        quarter = max(half // 2, 1)
-        own = me // 2
-        side = own // quarter
-        near = side * quarter + lax.rem(own + step, quarter)
-        far = (1 - side) * quarter + lax.rem(own + step, quarter)
-        return jnp.where(step < quarter, near, far) if half > 1 else own
-
-    def pipeline(step, carry):
-        @pl.when(step < half)
-        def _():
-            for place in range(2):
-                source = 2 * nth_pair(step) + place
-
-                @pl.when(source != me)
-                def _():
-                    for copy in arrivals(source):
-                        copy.wait_recv()
-
-                forward(source)
-
-        @pl.when(step > 0)
-        def _():
-            curl(nth_pair(step - 1))
-
-        return carry
-
-    lax.fori_loop(0, half + 1, pipeline, 0)
+    quarter = half // 2
+    near = me // half * quarter
+    far = quarter - near
+
+    def take(pair):
+        for place in range(2):
+            source = 2 * pair + place
+
+            @pl.when(source != me)
+            def _():
+                for copy in arrivals(source):
+                    copy.wait_recv()
+
+            forward(source)
+
+    def take_near(step, carry):
+        take(near + step)
+        return carry
+
+    def take_far(step, carry):
+        take(far + step)
+        curl(near + step)
+        return carry
+
+    def curl_far(step, carry):
+        curl(far + step)
+        return carry
+
+    lax.fori_loop(0, quarter, take_near, 0)
+    lax.fori_loop(0, quarter, take_far, 0)
+    lax.fori_loop(0, quarter, curl_far, 0)
 
     both = product(parts[:2 * total], parts[total:], ((1,), (1,)))
     crossed = both[:total, :total].T
@@ -399,26 +401,25 @@
 
     entries = summed[:, total:total + rank]
     maps = lead_all
-    gram = close(maps.T, close(summed[:, :total], maps))
+    gram = exact(maps.T, exact(summed[:, :total], maps))
     for turn in turns:
-        step_map = close(ortho_factor(gram, rank), turn)
-        gram = close(step_map.T, close(gram, step_map))
-        maps = close(maps, step_map)
+        step_map = exact(ortho_factor(gram, rank), turn)
+        gram = exact(step_map.T, exact(gram, step_map))
+        maps = exact(maps, step_map)
     factor = ortho_factor(gram, rank)
-    value = jnp.sum(factor * close(maps.T, entries), axis=0, keepdims=True)
-    norm_sq = jnp.sum(factor * close(gram, factor), axis=0, keepdims=True)
+    value = jnp.sum(factor * exact(entries.T, maps), axis=1, keepdims=True)
+    norm_sq = jnp.sum(factor * exact(factor, gram), axis=1, keepdims=True)
     cells_all = 3 * rows_y * spaces * plane
     floor = 0.5 * jnp.sqrt(norm_sq / cells_all + 1e-06)
     sign = value / jnp.maximum(jnp.abs(value), floor)
-    mix = close((factor * sign).T, maps, ((1,), (1,)))
+    mix = exact(factor, maps.T)
     mix_high, mix_low = split(mix)
     high = parts[total:2 * total]
     both = product(jnp.concatenate([mix_high, mix_low], axis=0), high)
-    out_ref[...] = both[:rank] + both[rank:] + product(mix_high, parts[:total])
+    out_ref[...] = (both[:rank] + both[rank:] + product(mix_high, parts[:total])) * sign
 
     def finish(step, carry):
-        for copy in copies(step):
-            copy.wait_send()
+        main_copy(step).wait_send()
         return carry
 
     lax.fori_loop(0, half, finish, 0)
@@ -435,6 +436,9 @@
         copy_c(step, sp).wait_send()
 
     def finish_halo(group, carry):
+        for side in range(2):
+            x_copy(side, group).wait_send()
+
         @pl.when(sp < spaces - 1)
         def _():
             halo_copy(0, group).wait_send()
@@ -465,20 +469,23 @@
     share = total // spaces
     lead_width = padded(rank * groups // 2, 128)
     vmem = pl.BlockSpec(memory_space=pltpu.VMEM)
-    smem = pl.BlockSpec(memory_space=pltpu.SMEM)
     dma = pltpu.SemaphoreType.DMA
     modes = pl.pallas_call(
         functools.partial(kernel, (groups, spaces)),
         out_shape=jax.ShapeDtypeStruct((rank, cells), F32),
-        in_specs=[pl.BlockSpec(memory_space=pltpu.HBM), vmem, smem, vmem, vmem, smem, smem],
+        in_specs=[pl.BlockSpec(memory_space=pltpu.HBM)] * 7,
         out_specs=vmem,
         scratch_shapes=[
             pltpu.VMEM(velocity.shape, BF16),
+            pltpu.VMEM(block_id.shape, jnp.int32),
+            pltpu.SMEM(metric.shape[::-1], F32),
+            pltpu.VMEM(leaf_rot.shape, F32),
+            pltpu.VMEM((merge_rot.shape[0], rank, 2 * rank), F32),
+            pltpu.SMEM(merge_order.shape, jnp.int32),
+            pltpu.SMEM(ref_cell.shape, jnp.int32),
             pltpu.VMEM((here * 3 * rows_y * cells_x, cells_z), F32),
-            pltpu.VMEM((groups, width_x, tile_rows, cells_z), BF16),
-            pltpu.VMEM((groups, 2, width_x + 2, tile_rows, cells_z), BF16),
-            pltpu.VMEM((groups, width_x, tile_rows, cells_z), BF16),
-            pltpu.VMEM((groups, 2, width_x + 2, tile_rows, cells_z), BF16),
+            pltpu.VMEM((groups, 3, width_x, tile_rows, cells_z), BF16),
+            pltpu.VMEM((groups, 3, width_x + 2, tile_rows, cells_z), BF16),
             pltpu.VMEM((2, groups, width_x, 2 * here, cells_z), BF16),
             pltpu.VMEM((2, groups, width_x, 2 * here, cells_z), BF16),
             pltpu.VMEM((groups, here, lead_width), F32),
@@ -489,14 +496,16 @@
             pltpu.VMEM((groups, share, gram_width), F32),
             pltpu.VMEM((spaces, share, gram_width), F32),
         ]
-        + [dma]
-        + [dma((groups,))] * 6
+        + [dma((7,))]
+        + [dma((groups,))] * 2
+        + [dma((2, groups))] * 2
+        + [dma((groups,))] * 2
         + [dma((2, groups))] * 2
         + [dma((spaces,))] * 2
         + [dma((groups,))] * 2
         + [dma((spaces,))] * 2,
         compiler_params=pltpu.CompilerParams(
-            collective_id=0, has_side_effects=True, vmem_limit_bytes=32 * 1024 * 1024
+            collective_id=0, has_side_effects=True, vmem_limit_bytes=56 * 1024 * 1024
         ),
     )(velocity, block_id, metric.T, leaf_rot, jnp.swapaxes(merge_rot, 1, 2), merge_order, ref_cell)
     return modes.reshape(rank, 3, rows_y, width_x * cells_z)

time: 42.2 us -> 41 us (0.972)
  local copies, waits for them, and re-layouts: 4.79 us -> 1.77 us
  Pallas kernels: 37 us -> 39 us
    unnamed x14 -> x0, local copies, waits for them, and re-layouts: 3.94 us -> none
    pallas_call x1, Pallas kernels: 37 us -> 39 us  [local(): pl.pallas_call(functools.partial(kernel, (groups, spaces)), out_shape=jax...]
    reshape x1, local copies, waits for them, and re-layouts: 0.84 us -> 1.77 us  [local(): return modes.reshape(rank, 3, rows_y, width_x * cells_z)]
where the time goes in v3:
time: 41 us; the launch traced here: 40.8 us
  Pallas kernels  39 us (95%)
  local copies, waits for them, and re-layouts  1.77 us (4%)
    pallas_call x1, Pallas kernels, local(): pl.pallas_call(functools.partial(kernel, (groups, spaces)), out_shape=jax...  39 us
    reshape x1, local copies, waits for them, and re-layouts, local(): return modes.reshape(rank, 3, rows_y, width_x * cells_z)  1.77 us

profile of v3, /device:TPU:0, one launch (start us, length us, event | category | flops | bytes accessed | tf_op | source)
XLA Modules:
  0.0 40.8 jit_solution(16001636225885577436)
XLA Ops:
  0.0 39.0 %shard_map.73 = f32[16,3072]{1,0:T(8,128)} custom-call(bf16[8,3,2,32,128]{4,3,2,1,0:T(8,128)(2,1)} %vel_hbm.1, s32[2,32,128]{2,1,0:T(8,128)} %block_hbm.1, f32[3,8]{1,0:T(4,128)} %bitcast.3, f32[1,8,16]{2,1,0:T(8,128)} %leaf_hbm.1, f32[7,16,32]{2,1,0:T(8,128)} %bitcast.2, s32[7]{0:T(128)} %order_hbm.1, s32[16]{0:T(128)} %cell_hbm.1), custom_call_target="tpu_custom_call" | custom-call | tf_op jit(solution)/shard_map/pallas_call | solution.py:473
  39.0 1.8 %reshape.3 = f32[16,3,2,512]{3,2,1,0:T(2,128)} reshape(f32[16,3072]{1,0:T(8,128)} %shard_map.73) | data formatting | bytes 393216 | tf_op jit(solution)/shard_map/reshape | solution.py:511

commit v4 on v3

--- a/solution.py
+++ b/solution.py
@@ -109,9 +109,9 @@
 
     def target(step):
         mine = me // half
-        far = (1 - mine) * half + lax.rem(me + step, half)
-        near = mine * half + lax.rem(me + step, half)
-        return jnp.where(step < half, far, near)
+        near = mine * half + lax.rem(me + step // 2, half)
+        far = (1 - mine) * half + lax.rem(me + step // 2, half)
+        return jnp.where(lax.rem(step, 2) == 0, near, far)
 
     def regroup(to, place):
         start = to * width_x
@@ -133,12 +133,12 @@
             sem_main_s.at[step], sem_main_r.at[me], device_id={"snap": target(step)}, device_id_type=MESH,
         )
 
-    def x_copy(side, group):
+    def x_copy(side, pair):
         from_row, to_row = (width_x, 0) if side == 0 else (1, width_x + 1)
         to = peer(1) if side == 0 else peer(groups - 1)
         return pltpu.make_async_remote_copy(
-            recv.at[group, pl.ds(1, 2), from_row], recv.at[group, pl.ds(1, 2), to_row],
-            sem_x_s.at[side, group], sem_x_r.at[side, group], device_id={"snap": to}, device_id_type=MESH,
+            recv.at[pl.ds(2 * pair, 2), pl.ds(1, 2), from_row], recv.at[pl.ds(2 * pair, 2), pl.ds(1, 2), to_row],
+            sem_x_s.at[side, pair], sem_x_r.at[side, pair], device_id={"snap": to}, device_id_type=MESH,
         )
 
     def arrivals(source):
@@ -158,8 +158,7 @@
         main_copy(step).start()
         return carry
 
-    lax.fori_loop(0, half, launch, 0)
-    lax.fori_loop(half + 1, groups, launch, 0)
+    lax.fori_loop(1, groups, launch, 0)
     regroup(me, recv.at[me, :, pl.ds(1, width_x)])
     for load in loads[1:]:
         load.wait()
@@ -180,30 +179,32 @@
 
     lax.fori_loop(1, groups, launch_lead, 0)
 
-    def halo_copy(side, group):
+    def halo_copy(side, pair):
         to = sp + 1 if side == 0 else sp - 1
         return pltpu.make_async_remote_copy(
-            stage.at[side, group], halo.at[side, group],
-            sem_halo_s.at[side, group], sem_halo_r.at[side, group],
+            stage.at[side, pl.ds(2 * pair, 2)], halo.at[side, pl.ds(2 * pair, 2)],
+            sem_halo_s.at[side, pair], sem_halo_r.at[side, pair],
             device_id={"space": to}, device_id_type=MESH,
         )
 
-    def forward(group):
+    def forward(pair):
         for side in range(2):
-            x_copy(side, group).start()
-        for x in range(width_x):
-            u_here = recv[group, 0, x + 1].astype(F32)
-            w_here = recv[group, 2, x + 1].astype(F32)
-            stage[1, group, x] = jnp.concatenate([u_here[:here], w_here[:here]], axis=0).astype(BF16)
-            stage[0, group, x] = jnp.concatenate([u_here[-here:], w_here[-here:]], axis=0).astype(BF16)
+            x_copy(side, pair).start()
+        for place in range(2):
+            group = 2 * pair + place
+            for x in range(width_x):
+                u_here = recv[group, 0, x + 1].astype(F32)
+                w_here = recv[group, 2, x + 1].astype(F32)
+                stage[1, group, x] = jnp.concatenate([u_here[:here], w_here[:here]], axis=0).astype(BF16)
+                stage[0, group, x] = jnp.concatenate([u_here[-here:], w_here[-here:]], axis=0).astype(BF16)
 
         @pl.when(sp < spaces - 1)
         def _():
-            halo_copy(0, group).start()
+            halo_copy(0, pair).start()
 
         @pl.when(sp > 0)
         def _():
-            halo_copy(1, group).start()
+            halo_copy(1, pair).start()
 
     @pl.when(sp == 0)
     def _():
@@ -263,23 +264,22 @@
         parts[pl.ds(start, 2 * here), pl.ds(column, cells_z)] = low
         parts[pl.ds(total + start, 2 * here), pl.ds(column, cells_z)] = high
 
-    def wait_halo(group):
+    def wait_halo(pair):
         for side in range(2):
-            x_copy(side, group).wait_recv()
+            x_copy(side, pair).wait_recv()
 
         @pl.when(sp > 0)
         def _():
-            halo_copy(0, group).wait_recv()
+            halo_copy(0, pair).wait_recv()
 
         @pl.when(sp < spaces - 1)
         def _():
-            halo_copy(1, group).wait_recv()
+            halo_copy(1, pair).wait_recv()
 
     def curl(pair):
         pair_groups = (2 * pair, 2 * pair + 1)
         start = pl.multiple_of(pair * 2 * here, 2 * here)
-        for group in pair_groups:
-            wait_halo(group)
+        wait_halo(pair)
 
         def load(ref, *index):
             both = [ref[(group, *index)].astype(F32) for group in pair_groups]
@@ -330,7 +330,7 @@
                 for copy in arrivals(source):
                     copy.wait_recv()
 
-            forward(source)
+        forward(pair)
 
     def take_near(step, carry):
         take(near + step)
@@ -422,8 +422,7 @@
         main_copy(step).wait_send()
         return carry
 
-    lax.fori_loop(0, half, finish, 0)
-    lax.fori_loop(half + 1, groups, finish, 0)
+    lax.fori_loop(1, groups, finish, 0)
 
     def finish_small(step, carry):
         lead_copy(step).wait_send()
@@ -435,21 +434,21 @@
         copy_a(step).wait_send()
         copy_c(step, sp).wait_send()
 
-    def finish_halo(group, carry):
+    def finish_halo(pair, carry):
         for side in range(2):
-            x_copy(side, group).wait_send()
+            x_copy(side, pair).wait_send()
 
         @pl.when(sp < spaces - 1)
         def _():
-            halo_copy(0, group).wait_send()
+            halo_copy(0, pair).wait_send()
 
         @pl.when(sp > 0)
         def _():
-            halo_copy(1, group).wait_send()
-
-        return carry
-
-    lax.fori_loop(0, groups, finish_halo, 0)
+            halo_copy(1, pair).wait_send()
+
+        return carry
+
+    lax.fori_loop(0, half, finish_halo, 0)
 
 
 def padded(size, unit):
@@ -498,9 +497,9 @@
         ]
         + [dma((7,))]
         + [dma((groups,))] * 2
-        + [dma((2, groups))] * 2
+        + [dma((2, groups // 2))] * 2
         + [dma((groups,))] * 2
-        + [dma((2, groups))] * 2
+        + [dma((2, groups // 2))] * 2
         + [dma((spaces,))] * 2
         + [dma((groups,))] * 2
         + [dma((spaces,))] * 2,

time: 41 us -> 40.6 us (level)
  no operation moved by 1% of the time
where the time goes in v4:
time: 40.6 us; the launch traced here: 40.4 us
  Pallas kernels  38.6 us (95%)
  local copies, waits for them, and re-layouts  1.77 us (4%)
    pallas_call x1, Pallas kernels, local(): pl.pallas_call(functools.partial(kernel, (groups, spaces)), out_shape=jax...  38.6 us
    reshape x1, local copies, waits for them, and re-layouts, local(): return modes.reshape(rank, 3, rows_y, width_x * cells_z)  1.77 us

profile of v4, /device:TPU:0, one launch (start us, length us, event | category | flops | bytes accessed | tf_op | source)
XLA Modules:
  0.0 40.4 jit_solution(8506108833165572565)
XLA Ops:
  0.0 38.6 %shard_map.73 = f32[16,3072]{1,0:T(8,128)} custom-call(bf16[8,3,2,32,128]{4,3,2,1,0:T(8,128)(2,1)} %vel_hbm.1, s32[2,32,128]{2,1,0:T(8,128)} %block_hbm.1, f32[3,8]{1,0:T(4,128)} %bitcast.3, f32[1,8,16]{2,1,0:T(8,128)} %leaf_hbm.1, f32[7,16,32]{2,1,0:T(8,128)} %bitcast.2, s32[7]{0:T(128)} %order_hbm.1, s32[16]{0:T(128)} %cell_hbm.1), custom_call_target="tpu_custom_call" | custom-call | tf_op jit(solution)/shard_map/pallas_call | solution.py:472
  38.6 1.8 %reshape.3 = f32[16,3,2,512]{3,2,1,0:T(2,128)} reshape(f32[16,3072]{1,0:T(8,128)} %shard_map.73) | data formatting | bytes 393216 | tf_op jit(solution)/shard_map/reshape | solution.py:510

commit v5 on v1

--- a/solution.py
+++ b/solution.py
@@ -21,6 +21,11 @@
     return lax.dot_general(left, right, (dims, ((), ())), preferred_element_type=F32)
 
 
+def split(value):
+    high = value.astype(BF16)
+    return high, (value - high.astype(F32)).astype(BF16)
+
+
 def iota(shape, dim):
     return lax.broadcasted_iota(jnp.int32, shape, dim)
 
@@ -30,33 +35,44 @@
     eye = iota(gram.shape, 0) == iota(gram.shape, 1)
     same = iota(gram.shape, 0) // rank == iota(gram.shape, 1) // rank
     diagonal = jnp.sum(jnp.where(eye, gram, 0.0), axis=0, keepdims=True)
-    if size > rank:
-        spread = jnp.broadcast_to(diagonal, (8, size))
-        trace = exact(spread, same.astype(F32))[:1]
-    else:
-        trace = jnp.sum(diagonal, axis=1, keepdims=True)
+    node_of = iota((1, size), 1) // rank
+    trace = jnp.zeros((1, size), F32)
+    for node in range(size // rank):
+        own = jnp.where(node_of == node, diagonal, 0.0)
+        trace = jnp.where(node_of == node, jnp.sum(own, axis=1, keepdims=True), trace)
     scale = (trace + 1e-06) / rank
     return 1.5 * eye.astype(F32) - jnp.where(same, 0.5 * gram / scale, 0.0)
 
 
 def kernel(
     dims,
-    vel_ref, block_ref, metric_ref, leaf_ref, rot_ref, order_ref, cell_ref, out_ref,
-    velf, send_u, send_vw, recv_u, recv_vw, stage, halo, lead, spacing, parts_hi, parts_lo,
+    vel_hbm, block_hbm, metric_hbm, leaf_hbm, rot_hbm, order_hbm, cell_hbm, out_ref,
+    vel_ref, block_ref, metric_ref, leaf_ref, rot_ref, order_ref, cell_ref,
+    velf, send_u, send_vw, recv_u, recv_vw, stage, halo, lead, spacing, parts,
     gram_own, gram_space, gram_snap, gram_all,
-    sem_u_s, sem_u_r, sem_vw_s, sem_vw_r, sem_lead_s, sem_lead_r, sem_halo_s, sem_halo_r,
+    sem_in, sem_u_s, sem_u_r, sem_vw_s, sem_vw_r, sem_lead_s, sem_lead_r, sem_halo_s, sem_halo_r,
     sem_a_s, sem_a_r, sem_b_s, sem_b_r, sem_c_s, sem_c_r,
 ):
     groups, spaces = dims
     here, _, rows_y, cells_x, cells_z = vel_ref.shape
     rank = leaf_ref.shape[2]
-    blocks = metric_ref.shape[0]
+    blocks = metric_ref.shape[1]
     total = groups * here
     width_x = cells_x // groups
     me = lax.axis_index("snap")
     sp = lax.axis_index("space")
     first_x = me * width_x
 
+    loads = [
+        pltpu.make_async_copy(source, place, sem_in.at[index])
+        for index, (source, place) in enumerate((
+            (vel_hbm, vel_ref), (block_hbm, block_ref), (metric_hbm, metric_ref), (leaf_hbm, leaf_ref),
+            (rot_hbm, rot_ref), (order_hbm, order_ref), (cell_hbm, cell_ref),
+        ))
+    ]
+    for load in loads:
+        load.start()
+
     def peer(step):
         return lax.rem(me + step, groups)
 
@@ -80,6 +96,7 @@
         velf[pl.ds(start, stretch), :] = vel_ref[snap].reshape(stretch, cells_z).astype(F32)
         return carry
 
+    loads[0].wait()
     lax.fori_loop(0, here, widen, 0)
 
     def tile(comp, x):
@@ -99,16 +116,6 @@
     for comp in range(2):
         send_vw[comp, 0] = send_vw[comp, cells_x]
         send_vw[comp, cells_x + 1] = send_vw[comp, 1]
-
-    lead_width = lead.shape[2]
-    turn = rot_ref[me // 2]
-    pick = (order_ref[me // 2] - me % 2).astype(F32)
-    pick = pick * pick
-    turn_own = turn[:rank] * (1.0 - pick) + turn[rank:] * pick
-    lead_own = exact(leaf_ref[0], turn_own)
-    repeat = (iota((rank, lead_width), 1) % rank == iota((rank, lead_width), 0)).astype(F32)
-    lead_wide = exact(lead_own, repeat)
-    lead[me] = jnp.where(iota(lead_wide.shape, 1) // rank == me // 2, lead_wide, 0.0)
 
     pl.semaphore_wait(barrier, groups + spaces - 2)
 
@@ -123,10 +130,6 @@
             pltpu.make_async_remote_copy(
                 send_u.at[pl.ds(start, width_x)], recv_u.at[me],
                 sem_u_s.at[step], sem_u_r.at[me], device_id={"snap": to}, device_id_type=MESH,
-            ),
-            pltpu.make_async_remote_copy(
-                lead.at[me], lead.at[me],
-                sem_lead_s.at[step], sem_lead_r.at[me], device_id={"snap": to}, device_id_type=MESH,
             ),
         )
 
@@ -153,6 +156,31 @@
 
     lax.fori_loop(1, groups, launch, 0)
 
+    for load in loads[1:]:
+        load.wait()
+
+    lead_width = lead.shape[2]
+    turn = rot_ref[me // 2].T
+    pick = (order_ref[me // 2] - me % 2).astype(F32)
+    pick = pick * pick
+    turn_own = turn[:rank] * (1.0 - pick) + turn[rank:] * pick
+    lead_own = exact(leaf_ref[0], turn_own)
+    repeat = (iota((rank, lead_width), 1) % rank == iota((rank, lead_width), 0)).astype(F32)
+    lead_wide = exact(lead_own, repeat)
+    lead[me] = jnp.where(iota(lead_wide.shape, 1) // rank == me // 2, lead_wide, 0.0)
+
+    def lead_copy(step):
+        return pltpu.make_async_remote_copy(
+            lead.at[me], lead.at[me],
+            sem_lead_s.at[step], sem_lead_r.at[me], device_id={"snap": peer(step)}, device_id_type=MESH,
+        )
+
+    def launch_lead(step, carry):
+        lead_copy(step).start()
+        return carry
+
+    lax.fori_loop(1, groups, launch_lead, 0)
+
     def halo_copy(side, group):
         to = sp + 1 if side == 0 else sp - 1
         return pltpu.make_async_remote_copy(
@@ -194,16 +222,12 @@
             for axis in range(3):
                 value = jnp.zeros((1, cells_z), F32)
                 for block in range(blocks):
-                    value = jnp.where(ids == block, metric_ref[block, axis], value)
+                    value = jnp.where(ids == block, metric_ref[axis, block], value)
                 spacing[axis, y, pl.ds(x, 1), :] = 0.5 * value
 
     plane = cells_x * cells_z
-    parts_hi[pl.ds(total, parts_hi.shape[0] - total), :] = jnp.zeros(
-        (parts_hi.shape[0] - total, parts_hi.shape[1]), BF16
-    )
-    parts_lo[pl.ds(total, parts_lo.shape[0] - total), :] = jnp.zeros(
-        (parts_lo.shape[0] - total, parts_lo.shape[1]), BF16
-    )
+    rest = parts.shape[0] - 2 * total
+    parts[pl.ds(2 * total, rest), :] = jnp.zeros((rest, parts.shape[1]), BF16)
     row = iota((rank, cells_z), 0)
     wanted = jnp.zeros((rank, cells_z), jnp.int32)
     for mode in range(rank):
@@ -214,7 +238,7 @@
                 base = ((comp * rows_y * spaces + sp * rows_y + y) * cells_x + first_x + x) * cells_z
                 hit = jnp.where(wanted == base + iota((rank, cells_z), 1), 1.0, 0.0)
                 column = ((comp * rows_y + y) * width_x + x) * cells_z
-                parts_hi[pl.ds(total, rank), pl.ds(column, cells_z)] = hit.astype(BF16)
+                parts[pl.ds(2 * total, rank), pl.ds(column, cells_z)] = hit.astype(BF16)
 
     depth = groups.bit_length() - 1
     turns = []
@@ -223,7 +247,7 @@
         stacked = []
         for k in range(nodes):
             node = groups - (groups >> level) + k
-            plain = rot_ref[node]
+            plain = rot_ref[node].T
             swapped = jnp.concatenate([plain[rank:], plain[:rank]], axis=0)
             flag = order_ref[node].astype(F32)
             stacked.append(plain * (1.0 - flag) + swapped * flag)
@@ -247,10 +271,9 @@
     lax.fori_loop(1, groups, receive, 0)
 
     def split_store(start, column, value):
-        high = value.astype(BF16)
-        low = (value - high.astype(F32)).astype(BF16)
-        parts_hi[pl.ds(start, 2 * here), pl.ds(column, cells_z)] = high
-        parts_lo[pl.ds(start, 2 * here), pl.ds(column, cells_z)] = low
+        high, low = split(value)
+        parts[pl.ds(start, 2 * here), pl.ds(column, cells_z)] = low
+        parts[pl.ds(total + start, 2 * here), pl.ds(column, cells_z)] = high
 
     def wait_halo(group):
         @pl.when(sp > 0)
@@ -306,12 +329,10 @@
 
     lax.fori_loop(0, groups // 2, curl, 0)
 
-    high = parts_hi[:total]
-    low = parts_lo[:total]
-    last = ((1,), (1,))
-    gram_own[...] = (
-        product(high, parts_hi[...], last) + product(low, parts_hi[...], last) + product(high, parts_lo[...], last)
-    ).reshape(gram_own.shape)
+    both = product(parts[:2 * total], parts[total:], ((1,), (1,)))
+    crossed = both[:total, :total].T
+    gap = jnp.zeros((total, both.shape[1] - total), F32)
+    gram_own[...] = (both[:total] + both[total:] + jnp.concatenate([crossed, gap], axis=1)).reshape(gram_own.shape)
 
     def copy_a(step):
         to = mate(step)
@@ -367,20 +388,20 @@
         gram = exact(step_map, exact(gram, step_map), first)
         maps = exact(maps, step_map)
     factor = ortho_factor(gram, rank)
-    value = jnp.sum(factor * exact(maps, entries, first), axis=0, keepdims=True)
-    norm_sq = jnp.sum(factor * exact(gram, factor), axis=0, keepdims=True)
+    value = jnp.sum(factor * exact(entries, maps, first), axis=1, keepdims=True)
+    norm_sq = jnp.sum(factor * exact(factor, gram), axis=1, keepdims=True)
     cells_all = 3 * rows_y * spaces * plane
     floor = 0.5 * jnp.sqrt(norm_sq / cells_all + 1e-06)
     sign = value / jnp.maximum(jnp.abs(value), floor)
-    mix = exact(factor * sign, maps, ((0,), (1,)))
-    mix_high = mix.astype(BF16)
-    mix_low = (mix - mix_high.astype(F32)).astype(BF16)
-    both = product(jnp.concatenate([mix_high, mix_low], axis=0), high)
-    out_ref[...] = both[:rank] + both[rank:] + product(mix_high, low)
+    mix = exact(factor, maps, ((1,), (1,)))
+    mix_high, mix_low = split(mix)
+    both = product(jnp.concatenate([mix_high, mix_low], axis=0), parts[total:2 * total])
+    out_ref[...] = (both[:rank] + both[rank:] + product(mix_high, parts[:total])) * sign
 
     def finish(step, carry):
         for copy in copies(step):
             copy.wait_send()
+        lead_copy(step).wait_send()
         copy_b(step).wait_send()
         return carry
 
@@ -420,14 +441,20 @@
     share = total // spaces
     lead_width = padded(rank * groups // 2, 128)
     vmem = pl.BlockSpec(memory_space=pltpu.VMEM)
-    smem = pl.BlockSpec(memory_space=pltpu.SMEM)
     dma = pltpu.SemaphoreType.DMA
     modes = pl.pallas_call(
         functools.partial(kernel, (groups, spaces)),
         out_shape=jax.ShapeDtypeStruct((rank, cells), F32),
-        in_specs=[vmem, vmem, smem, vmem, vmem, smem, smem],
+        in_specs=[pl.BlockSpec(memory_space=pltpu.HBM)] * 7,
         out_specs=vmem,
         scratch_shapes=[
+            pltpu.VMEM(velocity.shape, BF16),
+            pltpu.VMEM(block_id.shape, jnp.int32),
+            pltpu.SMEM(metric.shape[::-1], F32),
+            pltpu.VMEM(leaf_rot.shape, F32),
+            pltpu.VMEM((merge_rot.shape[0], rank, 2 * rank), F32),
+            pltpu.SMEM(merge_order.shape, jnp.int32),
+            pltpu.SMEM(ref_cell.shape, jnp.int32),
             pltpu.VMEM((here * 3 * rows_y * cells_x, cells_z), F32),
             pltpu.VMEM((cells_x, tile_rows, cells_z), BF16),
             pltpu.VMEM((2, cells_x + 2, tile_rows, cells_z), BF16),
@@ -437,22 +464,22 @@
             pltpu.VMEM((2, groups, width_x, 2 * here, cells_z), BF16),
             pltpu.VMEM((groups, here, lead_width), F32),
             pltpu.VMEM((3, rows_y, width_x, cells_z), F32),
-            pltpu.VMEM((gram_width, cells), BF16),
-            pltpu.VMEM((gram_width, cells), BF16),
+            pltpu.VMEM((total + gram_width, cells), BF16),
             pltpu.VMEM((spaces, share, gram_width), F32),
             pltpu.VMEM((spaces, share, gram_width), F32),
             pltpu.VMEM((groups, share, gram_width), F32),
             pltpu.VMEM((spaces, share, gram_width), F32),
         ]
+        + [dma((7,))]
         + [dma((groups,))] * 6
         + [dma((2, groups))] * 2
         + [dma((spaces,))] * 2
         + [dma((groups,))] * 2
         + [dma((spaces,))] * 2,
         compiler_params=pltpu.CompilerParams(
-            collective_id=0, has_side_effects=True, vmem_limit_bytes=32 * 1024 * 1024
+            collective_id=0, has_side_effects=True, vmem_limit_bytes=56 * 1024 * 1024
         ),
-    )(velocity, block_id, metric, leaf_rot, merge_rot, merge_order, ref_cell)
+    )(velocity, block_id, metric.T, leaf_rot, jnp.swapaxes(merge_rot, 1, 2), merge_order, ref_cell)
     return modes.reshape(rank, 3, rows_y, width_x * cells_z)
 
 

time: 41.9 us -> 39 us (0.931)
  local copies, waits for them, and re-layouts: 3.56 us -> 1.77 us
  Pallas kernels: 38 us -> 37 us
    unnamed x12 -> x0, local copies, waits for them, and re-layouts: 2.72 us -> none
    pallas_call x1, Pallas kernels: 38 us -> 37 us  [local(): pl.pallas_call(functools.partial(kernel, (groups, spaces)), out_shape=jax...]
    reshape x1, local copies, waits for them, and re-layouts: 0.84 us -> 1.77 us  [local(): return modes.reshape(rank, 3, rows_y, width_x * cells_z)]
where the time goes in v5:
time: 39 us; the launch traced here: 38.8 us
  Pallas kernels  37 us (95%)
  local copies, waits for them, and re-layouts  1.77 us (5%)
    pallas_call x1, Pallas kernels, local(): pl.pallas_call(functools.partial(kernel, (groups, spaces)), out_shape=jax...  37 us
    reshape x1, local copies, waits for them, and re-layouts, local(): return modes.reshape(rank, 3, rows_y, width_x * cells_z)  1.77 us

profile of v5, /device:TPU:0, one launch (start us, length us, event | category | flops | bytes accessed | tf_op | source)
XLA Modules:
  0.0 38.8 jit_solution(16214366642826128064)
XLA Ops:
  0.0 37.0 %shard_map.73 = f32[16,3072]{1,0:T(8,128)} custom-call(bf16[8,3,2,32,128]{4,3,2,1,0:T(8,128)(2,1)} %vel_hbm.1, s32[2,32,128]{2,1,0:T(8,128)} %block_hbm.1, f32[3,8]{1,0:T(4,128)} %bitcast.3, f32[1,8,16]{2,1,0:T(8,128)} %leaf_hbm.1, f32[7,16,32]{2,1,0:T(8,128)} %bitcast.2, s32[7]{0:T(128)} %order_hbm.1, s32[16]{0:T(128)} %cell_hbm.1), custom_call_target="tpu_custom_call" | custom-call | tf_op jit(solution)/shard_map/pallas_call | solution.py:445
  37.0 1.8 %reshape.3 = f32[16,3,2,512]{3,2,1,0:T(2,128)} reshape(f32[16,3072]{1,0:T(8,128)} %shard_map.73) | data formatting | bytes 393216 | tf_op jit(solution)/shard_map/reshape | solution.py:483

commit v6 on v5

--- a/solution.py
+++ b/solution.py
@@ -70,8 +70,7 @@
             (rot_hbm, rot_ref), (order_hbm, order_ref), (cell_hbm, cell_ref),
         ))
     ]
-    for load in loads:
-        load.start()
+    loads[0].start()
 
     def peer(step):
         return lax.rem(me + step, groups)
@@ -88,6 +87,8 @@
         return carry
 
     lax.fori_loop(1, groups, greet, 0)
+    for load in loads[1:]:
+        load.start()
 
     stretch = 3 * rows_y * cells_x
 
@@ -395,8 +396,16 @@
     sign = value / jnp.maximum(jnp.abs(value), floor)
     mix = exact(factor, maps, ((1,), (1,)))
     mix_high, mix_low = split(mix)
-    both = product(jnp.concatenate([mix_high, mix_low], axis=0), parts[total:2 * total])
-    out_ref[...] = (both[:rank] + both[rank:] + product(mix_high, parts[:total])) * sign
+    upper = jnp.concatenate([mix_high, mix_high], axis=1)
+    lower = jnp.concatenate([jnp.zeros_like(mix_low), mix_low], axis=1)
+    both = product(jnp.concatenate([upper, lower], axis=0), parts[:2 * total])
+    modes = (both[:rank] + both[rank:]) * sign
+    for comp in range(3):
+        for x in range(width_x):
+            for y in range(rows_y):
+                column = ((comp * rows_y + y) * width_x + x) * cells_z
+                row = (comp * width_x + x) * rows_y + y
+                out_ref[pl.ds(row, rank, stride=3 * width_x * rows_y), :] = modes[:, column:column + cells_z]
 
     def finish(step, carry):
         for copy in copies(step):
@@ -444,7 +453,7 @@
     dma = pltpu.SemaphoreType.DMA
     modes = pl.pallas_call(
         functools.partial(kernel, (groups, spaces)),
-        out_shape=jax.ShapeDtypeStruct((rank, cells), F32),
+        out_shape=jax.ShapeDtypeStruct((rank * cells // cells_z, cells_z), F32),
         in_specs=[pl.BlockSpec(memory_space=pltpu.HBM)] * 7,
         out_specs=vmem,
         scratch_shapes=[
@@ -480,7 +489,8 @@
             collective_id=0, has_side_effects=True, vmem_limit_bytes=56 * 1024 * 1024
         ),
     )(velocity, block_id, metric.T, leaf_rot, jnp.swapaxes(merge_rot, 1, 2), merge_order, ref_cell)
-    return modes.reshape(rank, 3, rows_y, width_x * cells_z)
+    modes = modes.reshape(rank, 3, width_x, rows_y, cells_z)
+    return jnp.swapaxes(modes, 2, 3).reshape(rank, 3, rows_y, width_x * cells_z)
 
 
 def solution(mesh):

time: 39 us -> 38.8 us (level)
    reshape x1 -> x0, local copies, waits for them, and re-layouts: 1.77 us -> none  [local(): return modes.reshape(rank, 3, rows_y, width_x * cells_z)]
    unnamed x0 -> x1, local copies, waits for them, and re-layouts: none -> 1.62 us
where the time goes in v6:
time: 38.8 us; the launch traced here: 38.6 us
  Pallas kernels  37 us (95%)
  local copies, waits for them, and re-layouts  1.62 us (4%)
    pallas_call x1, Pallas kernels, local(): pl.pallas_call(functools.partial(kernel, (groups, spaces)), out_shape=jax...  37 us
    unnamed x1, local copies, waits for them, and re-layouts  1.62 us

profile of v6, /device:TPU:0, one launch (start us, length us, event | category | flops | bytes accessed | tf_op | source)
XLA Modules:
  0.0 38.6 jit_solution(2148406710332235544)
XLA Ops:
  0.0 37.0 %shard_map.73 = f32[384,128]{1,0:T(8,128)} custom-call(bf16[8,3,2,32,128]{4,3,2,1,0:T(8,128)(2,1)} %vel_hbm.1, s32[2,32,128]{2,1,0:T(8,128)} %block_hbm.1, f32[3,8]{1,0:T(4,128)} %bitcast.9, f32[1,8,16]{2,1,0:T(8,128)} %leaf_hbm.1, f32[7,16,32]{2,1,0:T(8,128)} %bitcast.8, s32[7]{0:T(128)} %order_hbm.1, s32[16]{0:T(128)} %cell_hbm.1), custom_call_target="tpu_custom_call" | custom-call | tf_op jit(solution)/shard_map/pallas_call | solution.py:454
  37.0 1.6 %copy.10 = f32[16,3,2,512]{3,2,1,0:T(2,128)} copy(f32[16,3,2,512]{3,2,1,0:T(2,128)} %bitcast.7) | data formatting | bytes 393216

commit v7 on v6

--- a/solution.py
+++ b/solution.py
@@ -108,7 +108,6 @@
         return jnp.concatenate(pieces, axis=0).astype(BF16)
 
     def regroup(x, carry):
-        send_u[x] = tile(0, x)
         send_vw[0, x + 1] = tile(1, x)
         send_vw[1, x + 1] = tile(2, x)
         return carry
@@ -119,6 +118,10 @@
         send_vw[comp, cells_x + 1] = send_vw[comp, 1]
 
     pl.semaphore_wait(barrier, groups + spaces - 2)
+
+    def regroup_u(x, carry):
+        send_u[x] = tile(0, x)
+        return carry
 
     def copies(step):
         to = peer(step)
@@ -150,12 +153,17 @@
             ),
         )
 
-    def launch(step, carry):
-        for copy in copies(step):
-            copy.start()
-        return carry
-
-    lax.fori_loop(1, groups, launch, 0)
+    def launch_vw(step, carry):
+        copies(step)[0].start()
+        return carry
+
+    def launch_u(step, carry):
+        copies(step)[1].start()
+        return carry
+
+    lax.fori_loop(1, groups, launch_vw, 0)
+    lax.fori_loop(0, cells_x, regroup_u, 0, unroll=4)
+    lax.fori_loop(1, groups, launch_u, 0)
 
     for load in loads[1:]:
         load.wait()

time: 38.8 us -> 38.8 us (level)
  no operation moved by 1% of the time
where the time goes in v7:
time: 38.8 us; the launch traced here: 38.6 us
  Pallas kernels  37 us (95%)
  local copies, waits for them, and re-layouts  1.62 us (4%)
    pallas_call x1, Pallas kernels, local(): pl.pallas_call(functools.partial(kernel, (groups, spaces)), out_shape=jax...  37 us
    unnamed x1, local copies, waits for them, and re-layouts  1.62 us

profile of v7, /device:TPU:0, one launch (start us, length us, event | category | flops | bytes accessed | tf_op | source)
XLA Modules:
  0.0 38.6 jit_solution(4792232244663443959)
XLA Ops:
  0.0 37.0 %shard_map.73 = f32[384,128]{1,0:T(8,128)} custom-call(bf16[8,3,2,32,128]{4,3,2,1,0:T(8,128)(2,1)} %vel_hbm.1, s32[2,32,128]{2,1,0:T(8,128)} %block_hbm.1, f32[3,8]{1,0:T(4,128)} %bitcast.9, f32[1,8,16]{2,1,0:T(8,128)} %leaf_hbm.1, f32[7,16,32]{2,1,0:T(8,128)} %bitcast.8, s32[7]{0:T(128)} %order_hbm.1, s32[16]{0:T(128)} %cell_hbm.1), custom_call_target="tpu_custom_call" | custom-call | tf_op jit(solution)/shard_map/pallas_call | solution.py:462
  37.0 1.6 %copy.10 = f32[16,3,2,512]{3,2,1,0:T(2,128)} copy(f32[16,3,2,512]{3,2,1,0:T(2,128)} %bitcast.7) | data formatting | bytes 393216

commit v8 on v6

--- a/solution.py
+++ b/solution.py
@@ -98,7 +98,7 @@
         return carry
 
     loads[0].wait()
-    lax.fori_loop(0, here, widen, 0)
+    lax.fori_loop(0, here, widen, 0, unroll=2)
 
     def tile(comp, x):
         pieces = [
@@ -113,7 +113,7 @@
         send_vw[1, x + 1] = tile(2, x)
         return carry
 
-    lax.fori_loop(0, cells_x, regroup, 0, unroll=4)
+    lax.fori_loop(0, cells_x, regroup, 0, unroll=8)
     for comp in range(2):
         send_vw[comp, 0] = send_vw[comp, cells_x]
         send_vw[comp, cells_x + 1] = send_vw[comp, 1]

time: 38.8 us -> 38.8 us (level)
  no operation moved by 1% of the time
where the time goes in v8:
time: 38.8 us; the launch traced here: 38.6 us
  Pallas kernels  37 us (95%)
  local copies, waits for them, and re-layouts  1.62 us (4%)
    pallas_call x1, Pallas kernels, local(): pl.pallas_call(functools.partial(kernel, (groups, spaces)), out_shape=jax...  37 us
    unnamed x1, local copies, waits for them, and re-layouts  1.62 us

profile of v8, /device:TPU:0, one launch (start us, length us, event | category | flops | bytes accessed | tf_op | source)
XLA Modules:
  0.0 38.6 jit_solution(10679957327564264656)
XLA Ops:
  0.0 37.0 %shard_map.73 = f32[384,128]{1,0:T(8,128)} custom-call(bf16[8,3,2,32,128]{4,3,2,1,0:T(8,128)(2,1)} %vel_hbm.1, s32[2,32,128]{2,1,0:T(8,128)} %block_hbm.1, f32[3,8]{1,0:T(4,128)} %bitcast.9, f32[1,8,16]{2,1,0:T(8,128)} %leaf_hbm.1, f32[7,16,32]{2,1,0:T(8,128)} %bitcast.8, s32[7]{0:T(128)} %order_hbm.1, s32[16]{0:T(128)} %cell_hbm.1), custom_call_target="tpu_custom_call" | custom-call | tf_op jit(solution)/shard_map/pallas_call | solution.py:454
  37.0 1.6 %copy.10 = f32[16,3,2,512]{3,2,1,0:T(2,128)} copy(f32[16,3,2,512]{3,2,1,0:T(2,128)} %bitcast.7) | data formatting | bytes 393216
